TPU v7x, 32 devices: a whole 2x2x4 slice. The times are simulated.
32 devices in a mesh: seq: 16 (over z, y, core), grp: 2 (over x).
Axes of the slice: x: 2, y: 2, z: 4, core: 2. Of those that a mesh axis runs over, the one named last changes fastest.
Arguments:
- prompt_tokens: bfloat16 [16384, 2048], P('seq'), may hold values from -6 to 6
- response_tokens: bfloat16 [2, 16, 256, 2048], P('grp', 'seq'), may hold values from -6 to 6
- w_query: bfloat16 [2048, 1024], P('seq', 'grp'), may hold values from -0.125 to 0.125
- w_key: bfloat16 [2048, 1024], P('seq', 'grp'), may hold values from -0.125 to 0.125
- w_value: bfloat16 [2048, 2048], P('seq', 'grp'), may hold values from -0.125 to 0.125
- w_decay: bfloat16 [2048, 16], P('seq', 'grp'), may hold values from -0.125 to 0.125
- w_beta: bfloat16 [2048, 16], P('seq', 'grp'), may hold values from -0.125 to 0.125
- decay_rate: float32 [16], replicated, may hold values from 0 to 0.06
- beta_shift: float32 [16], replicated, may hold values from -9 to 1
- out_gain: float32 [128], replicated, may hold values from 0.25 to 1.75
- resp_lengths: int32 [2, 16], P('grp', 'seq'), may hold values from 1 to 256, 2048 in all within a row
Outputs:
- prompt_output: bfloat16 [16384, 2048], P('seq', 'grp')
- response_output: bfloat16 [2, 16, 256, 2048], P('grp', 'seq')
Inputs may be any that keep to these rules, and one draw needn't show every extreme that they name: `resp_lengths`: in every group one response has exactly 256 tokens, and a group's lengths sum to 2048.
All inputs are finite; a program needn't handle non-finite values.
Results may differ from a plain program's by a relative error of at most 0.0062.
Values may be sent and summed in bfloat16 or wider, within the bound.
A program may use at most 128 MiB of HBM per device.

v0:
```python
import jax
import jax.numpy as jnp
from jax import lax
from jax.sharding import PartitionSpec as P

DK = 128
SPAN = 64


def make_heads(raw, rate, shift):
    count = raw[0].shape[0]
    key_heads = raw[0].shape[1] // DK
    value_heads = raw[3].shape[1]
    repeat = value_heads // key_heads
    query_rows = raw[0].reshape(count, key_heads, DK)
    keys = raw[1].reshape(count, key_heads, DK)
    query_rows = (
        query_rows
        * lax.rsqrt(jnp.sum(query_rows * query_rows, axis=-1, keepdims=True) + 1e-06)
        * DK ** (-0.5)
    )
    keys = keys * lax.rsqrt(jnp.sum(keys * keys, axis=-1, keepdims=True) + 1e-06)
    query_rows = jnp.repeat(query_rows.astype(jnp.bfloat16), repeat, axis=1)
    keys = jnp.repeat(keys.astype(jnp.bfloat16), repeat, axis=1)
    values = raw[2].reshape(count, value_heads, raw[2].shape[1] // value_heads).astype(jnp.bfloat16)
    log_decay = -rate * jax.nn.softplus(raw[3])
    beta = jax.nn.sigmoid(raw[4] + shift)
    return (query_rows, keys, values, log_decay, beta)


def finish(layer_output, gain):
    normed = (
        layer_output
        * lax.rsqrt(jnp.mean(layer_output * layer_output, axis=-1, keepdims=True) + 1e-06)
        * gain
    )
    return normed.reshape(normed.shape[0], normed.shape[1] * normed.shape[2]).astype(jnp.bfloat16)


def invert_unit(lower):
    highest_level = lax.Precision.HIGHEST
    size = lower.shape[-1]
    ident = jnp.eye(size, dtype=jnp.float32)
    power = -lower
    inverse = ident + power
    for level in range(size.bit_length() - 2):
        power = jnp.einsum("hij,hjl->hil", power, power, precision=highest_level)
        inverse = jnp.einsum("hij,hjl->hil", inverse, ident + power, precision=highest_level)
    return inverse


def span_core(query_rows, keys, values, log_decay, beta, state_matrix, track):
    highest_level = lax.Precision.HIGHEST
    size = query_rows.shape[0]
    width = values.shape[2]
    query_float = query_rows.astype(jnp.float32)
    key_float = keys.astype(jnp.float32)
    value_float = values.astype(jnp.float32)
    cumul = jnp.cumsum(log_decay, axis=0)
    decay_factor = jnp.exp(cumul)
    row = lax.broadcasted_iota(jnp.int32, (size, size), 0)
    column = lax.broadcasted_iota(jnp.int32, (size, size), 1)
    within = row >= column
    strict = row > column
    by_head = cumul.T
    spread = by_head[:, :, None] - by_head[:, None, :]
    decay = jnp.where(within, jnp.exp(jnp.where(within, spread, 0.0)), 0.0)
    key_dots = jnp.einsum("ihk,jhk->hij", keys, keys, preferred_element_type=jnp.float32)
    lower = jnp.where(strict, beta.T[:, :, None] * decay * key_dots, 0.0)
    inverse = invert_unit(lower)
    rhs = jnp.concatenate(
        [beta[..., None] * value_float, (beta * decay_factor)[..., None] * key_float], axis=2
    )
    solved = jnp.einsum("hij,jhc->ihc", inverse, rhs, precision=highest_level)
    fresh_value = solved[..., :width]
    key_weights = solved[..., width:]
    delta_update = fresh_value - jnp.einsum(
        "wuq,uqn->wun", key_weights, state_matrix, precision=highest_level
    )
    scores = decay * jnp.einsum(
        "ihk,jhk->hij", query_rows, keys, preferred_element_type=jnp.float32
    )
    layer_output = decay_factor[..., None] * jnp.einsum(
        "wuq,uqn->wun", query_float, state_matrix, precision=highest_level
    )
    layer_output = layer_output + jnp.einsum(
        "hij,jhv->ihv", scores, delta_update, precision=highest_level
    )
    tail_tokens = jnp.exp(cumul[-1:] - cumul)[..., None] * key_float
    last_token = decay_factor[-1][:, None, None]
    state_updated = last_token * state_matrix + jnp.einsum(
        "cwx,cwq->wxq", tail_tokens, delta_update, precision=highest_level
    )
    if track is None:
        return (layer_output, state_updated, None, None)
    ident = jnp.eye(keys.shape[2], dtype=jnp.float32)
    transit_state = last_token * ident - jnp.einsum(
        "ihk,ihj->hkj", tail_tokens, key_weights, precision=highest_level
    )
    weighted = decay_factor[..., None] * query_float - jnp.einsum(
        "hij,jhk->ihk", scores, key_weights, precision=highest_level
    )
    lifted = jnp.einsum("ihk,hkj->ihj", weighted, track, precision=highest_level)
    track_new = jnp.einsum("hkj,hjl->hkl", transit_state, track, precision=highest_level)
    return (layer_output, state_updated, lifted, track_new)


def block_pass(query_rows, keys, values, log_decay, beta, state_matrix, tracking):
    count = query_rows.shape[0]
    heads = query_rows.shape[1]
    blocks = count // SPAN
    pieces = tuple(
        (
            a.reshape((blocks, SPAN) + a.shape[1:])
            for a in (query_rows, keys, values, log_decay, beta)
        )
    )
    if tracking:
        ident = jnp.broadcast_to(jnp.eye(DK, dtype=jnp.float32), (heads, DK, DK))

        def block_advance(carry, piece):
            layer_output, state_updated, lifted, track_new = span_core(
                piece[0], piece[1], piece[2], piece[3], piece[4], carry[0], carry[1]
            )
            return ((state_updated, track_new), (layer_output, lifted))

        (state_matrix, transit_state), (outs, lifted) = lax.scan(
            block_advance, (state_matrix, ident), pieces
        )
        return (
            outs.reshape(count, heads, outs.shape[-1]),
            lifted.reshape(count, heads, DK),
            state_matrix,
            transit_state,
        )

    def plain(carry, piece):
        layer_output, state_updated, unused, unused_too = span_core(
            piece[0], piece[1], piece[2], piece[3], piece[4], carry, None
        )
        return (state_updated, layer_output)

    state_matrix, outs = lax.scan(plain, state_matrix, pieces)
    return (outs.reshape(count, heads, outs.shape[-1]), None, state_matrix, None)


def response_pass(query_rows, keys, values, log_decay, beta, state_matrix, live):
    n_live = (live + SPAN - 1) // SPAN
    buffer = jnp.zeros(values.shape, jnp.float32)

    def response_advance(index, carry):
        state_matrix, buffer = carry
        offset = index * SPAN
        piece = tuple(
            (
                lax.dynamic_slice_in_dim(a, offset, SPAN, 0)
                for a in (query_rows, keys, values, log_decay, beta)
            )
        )
        layer_output, state_matrix, unused, unused_too = span_core(
            piece[0], piece[1], piece[2], piece[3], piece[4], state_matrix, None
        )
        buffer = lax.dynamic_update_slice_in_dim(buffer, layer_output, offset, 0)
        return (state_matrix, buffer)

    state_matrix, buffer = lax.fori_loop(0, n_live, response_advance, (state_matrix, buffer))
    return buffer


def adder(left, pieces):
    return tuple((jnp.dot(left, p, preferred_element_type=jnp.float32) for p in pieces))


def apply_map(transit_state, state_matrix):
    return jnp.einsum("ist,ite->ise", transit_state, state_matrix, precision=lax.Precision.HIGHEST)


def shards(
    prompt_tokens,
    response_tokens,
    w_query,
    w_key,
    w_value,
    w_decay,
    w_beta,
    decay_rate,
    beta_shift,
    out_gain,
    resp_lengths,
):
    weights = (w_query, w_key, w_value, w_decay, w_beta)
    local_heads = w_decay.shape[1]
    first_head = lax.axis_index("grp") * local_heads
    rate_local = lax.dynamic_slice_in_dim(decay_rate, first_head, local_heads)
    shift_local = lax.dynamic_slice_in_dim(beta_shift, first_head, local_heads)
    tokens = response_tokens.reshape(response_tokens.shape[2], response_tokens.shape[3])
    length = tokens.shape[0]
    prompt_raw = adder(
        prompt_tokens,
        (
            lax.all_gather(weights[0], "seq", axis=0, tiled=True),
            lax.all_gather(weights[1], "seq", axis=0, tiled=True),
            lax.all_gather(weights[2], "seq", axis=0, tiled=True),
            lax.all_gather(weights[3], "seq", axis=0, tiled=True),
            lax.all_gather(weights[4], "seq", axis=0, tiled=True),
        ),
    )
    columns = (
        lax.all_gather(weights[0], "grp", axis=1, tiled=True),
        lax.all_gather(weights[1], "grp", axis=1, tiled=True),
        lax.all_gather(weights[2], "grp", axis=1, tiled=True),
        lax.all_gather(weights[3], "grp", axis=1, tiled=True),
        lax.all_gather(weights[4], "grp", axis=1, tiled=True),
    )
    resp_raw = adder(
        tokens,
        (
            lax.all_gather(columns[0], "seq", axis=0, tiled=True),
            lax.all_gather(columns[1], "seq", axis=0, tiled=True),
            lax.all_gather(columns[2], "seq", axis=0, tiled=True),
            lax.all_gather(columns[3], "seq", axis=0, tiled=True),
            lax.all_gather(columns[4], "seq", axis=0, tiled=True),
        ),
    )
    query_rows, keys, values, log_decay, beta = make_heads(prompt_raw, rate_local, shift_local)
    zero_state = jnp.zeros((local_heads, DK, values.shape[2]), jnp.float32)
    out_local, lifted, local_end, transit_state = block_pass(
        query_rows, keys, values, log_decay, beta, zero_state, True
    )
    all_maps, all_ends = (
        lax.all_gather(transit_state[None], "seq", axis=0, tiled=True),
        lax.all_gather(local_end[None], "seq", axis=0, tiled=True),
    )

    def body_advance(state_matrix, pieces):
        return (apply_map(pieces[0], state_matrix) + pieces[1], state_matrix)

    end, starts = lax.scan(body_advance, zero_state, (all_maps, all_ends))
    start = lax.dynamic_index_in_dim(starts, lax.axis_index("seq"), 0, keepdims=False)
    prompt_out, unused, unused_end, unused_map = block_pass(
        query_rows, keys, values, log_decay, beta, start, False
    )
    prompt_output = finish(prompt_out, out_gain)
    live = resp_lengths.reshape(())
    positions = lax.broadcasted_iota(jnp.int32, (length, 1), 0)
    heads_end = lax.all_gather(end, "grp", axis=0, tiled=True)
    r_query, r_keys, r_values, r_decay, r_beta = make_heads(resp_raw, decay_rate, beta_shift)
    resp_out = response_pass(r_query, r_keys, r_values, r_decay, r_beta, heads_end, live)
    finished = finish(resp_out, out_gain)
    masked = jnp.where(positions < live, finished, jnp.zeros_like(finished))
    return (prompt_output, masked.reshape(1, 1, length, masked.shape[1]))


def solution(mesh):
    placed = (
        P("seq", None),
        P("grp", "seq", None, None),
        P("seq", "grp"),
        P("seq", "grp"),
        P("seq", "grp"),
        P("seq", "grp"),
        P("seq", "grp"),
        P(),
        P(),
        P(),
        P("grp", "seq"),
    )
    return jax.shard_map(
        shards,
        mesh=mesh,
        in_specs=placed,
        out_specs=(P("seq", "grp"), P("grp", "seq", None, None)),
        check_vma=False,
    )
```

profile of v0, /device:TPU:8, one launch (start us, length us, event | category | flops | bytes accessed | tf_op | source)
XLA Modules:
  0.0 865.4 jit_solution(5162636740084316550)
XLA Ops:
  9.4 7.6 all_gather.64
  17.1 6.0 all_gather.70
  23.1 9.1 %all_gather.68 = bf16[128,2048]{1,0:T(8,128)(2,1)} all-gather(bf16[128,1024]{1,0:T(8,128)(2,1)} %param.23), channel_id=1, replica_groups=mesh['seq'=16,'grp'=2] {'grp'}, dimensions={1}, use_global_device_ids=true | all-gather | bytes 786432 | tf_op jit(solution)/shard_map/all_gather | solution.py:211
  32.3 19.6 %all_gather.54 = bf16[2048,8]{0,1:T(8,128)(2,1)S(1)} all-gather(bf16[128,8]{0,1:T(8,128)(2,1)} %param.24), channel_id=1, replica_groups=mesh['seq'=16,'grp'=2] {'seq'}, dimensions={0}, use_global_device_ids=true | all-gather | bytes 34816 | tf_op jit(solution)/shard_map/all_gather | solution.py:204
  52.6 3.4 fusion.141
  57.0 17.5 %all_gather.56 = bf16[2048,8]{0,1:T(8,128)(2,1)S(1)} all-gather(bf16[128,8]{0,1:T(8,128)(2,1)S(1)} %copy-done.11), channel_id=1, replica_groups=mesh['seq'=16,'grp'=2] {'seq'}, dimensions={0}, use_global_device_ids=true | all-gather | bytes 34816 | tf_op jit(solution)/shard_map/all_gather | solution.py:205
  74.6 3.4 fusion.127
  78.2 5.3 multiply_reduce_fusion.3
  88.1 16.4 %all-gather.14.cloned.1.call-done = bf16[2048,1024]{1,0:T(8,128)(2,1)} async-done(((bf16[128,1024]{1,0:T(8,128)(2,1)}), bf16[2048,1024]{1,0:T(8,128)(2,1)}) %all-gather.14.cloned.1.call-update) | async-done | bytes 4194320 | tf_op jit(solution)/shard_map/all_gather | solution.py:203
  104.4 8.0 convert_bitcast_fusion
  115.0 218.2 %while.52 = (s32[]{:T(128)}, f32[8,128,128]{2,1,0:T(8,128)S(1)}, f32[8,128,128]{2,1,0:T(8,128)S(1)}, f32[16,64,8]{2,1,0:T(8,128)}, bf16[16,64,8,128]{3,1,2,0:T(8...) while((s32[]{:T(128)}, f32[8,128,128]{2,1,0:T(8,128)S(1)}, ...), condition=%wide.region_3.4_spmd.clone, body=%wide.region_1.3_spmd.clone.sunk | while | flops 866042368 | bytes 12118872 | solution.py:127
  124.1 2.0 convolution_add_fusion.21
  137.7 2.0 convolution_add_fusion.21
  151.3 2.0 convolution_add_fusion.21
  178.5 2.0 convolution_add_fusion.21
  192.1 2.0 convolution_add_fusion.21
  205.8 2.0 convolution_add_fusion.21
  219.4 2.0 convolution_add_fusion.21
  233.1 2.0 convolution_add_fusion.21
  246.7 2.0 convolution_add_fusion.21
  335.6 4.3 all_gather.62
  339.9 4.3 all_gather.66
  344.3 16.6 %all_gather.63 = bf16[2048,16]{0,1:T(8,128)(2,1)S(1)} all-gather(bf16[128,16]{0,1:T(8,128)(2,1)S(1)} %all_gather.62), channel_id=1, replica_groups=mesh['seq'=16,'grp'=2] {'seq'}, dimensions={0}, use_global_device_ids=true | all-gather | bytes 69632 | tf_op jit(solution)/shard_map/all_gather | solution.py:221
  360.9 18.6 %all_gather.67 = bf16[2048,16]{0,1:T(8,128)(2,1)S(1)} all-gather(bf16[128,16]{0,1:T(8,128)(2,1)S(1)} %all_gather.66), channel_id=1, replica_groups=mesh['seq'=16,'grp'=2] {'seq'}, dimensions={0}, use_global_device_ids=true | all-gather | bytes 69632 | tf_op jit(solution)/shard_map/all_gather | solution.py:222
  380.3 5.3 multiply_reduce_fusion.2
  388.6 6.5 copy.164
  395.1 3.5 multiply_reduce_fusion.5
  399.5 2.1 copy.165
  401.6 6.6 copy.167
  408.2 3.5 multiply_reduce_fusion.4
  412.6 2.0 copy.168
  414.6 12.4 %copy.166 = bf16[2048,2048]{1,0:T(8,128)(2,1)} copy(bf16[2048,2048]{0,1:T(8,128)(2,1)} %bitcast.459) | data formatting | bytes 16777216 | tf_op jit(solution)/shard_map/dot_general | solution.py:171
  427.0 5.9 convolution_convert_fusion
  432.9 50.3 %all-gather.28.cloned.1.call-done = f32[128,128,128]{2,1,0:T(8,128)} async-done(((f32[8,128,128]{2,1,0:T(8,128)}), f32[128,128,128]{2,1,0:T(8,128)}) %all-gather.28.cloned.1.call-update) | async-done | bytes 8388624 | tf_op jit(solution)/shard_map/all_gather | solution.py:232
  483.2 44.2 %while.53 = (s32[]{:T(128)}, f32[8,128,128]{2,1,0:T(8,128)S(1)}, f32[16,8,128,128]{3,2,1,0:T(8,128)}, f32[16,8,128,128]{3,2,1,0:T(8,128)}, f32[16,8,128,128]{3,2,1,0:T(8,128)}, /*index=5*/s32[]{:T(128)}, s32[]{:T(128)}) while((s32[]{:T(128)}, f32[8,128,128]{2,1,0:T(8,128)S(1)}, f32[16,8,128,128]{3,2,1,0:T(8,128)}, ...), condition=%wide.region_5.6_spmd.clone, body=%wide.region_4.5_spmd.clone.sunk | while | flops 201719808 | bytes 4195939 | solution.py:238
  531.0 233.4 %while.50 = (s32[]{:T(128)}, f32[8,128,128]{2,1,0:T(8,128)S(1)}, f32[16,64,8,128]{3,1,2,0:T(8,128)}, f32[16,64,8]{2,1,0:T(8,128)}, bf16[16,64,8,128]{3,1,2,0:T(8...) while((s32[]{:T(128)}, f32[8,128,128]{2,1,0:T(8,128)S(1)}, ...), condition=%wide.region_9.10_spmd, body=%wide.region_7.9_spmd.sunk | while | flops 723010048 | bytes 10696017 | solution.py:143
  541.3 2.1 convolution_add_fusion.17
  555.9 2.1 convolution_add_fusion.17
  570.5 2.1 convolution_add_fusion.17
  585.1 2.1 convolution_add_fusion.17
  599.6 2.1 convolution_add_fusion.17
  614.2 2.1 convolution_add_fusion.17
  628.8 2.1 convolution_add_fusion.17
  643.3 2.1 convolution_add_fusion.17
  657.9 2.1 convolution_add_fusion.17
  672.5 2.1 convolution_add_fusion.17
  687.0 2.1 convolution_add_fusion.17
  701.6 2.1 convolution_add_fusion.17
  716.2 2.1 convolution_add_fusion.17
  730.7 2.1 convolution_add_fusion.17
  745.3 2.1 convolution_add_fusion.17
  759.8 2.1 convolution_add_fusion.17
  764.4 7.6 copy.161
  775.6 2.7 fusion.123
  781.2 70.6 %while.51 = (s32[]{:T(128)}, f32[16,128,128]{2,1,0:T(8,128)S(1)}, f32[256,16,128]{2,0,1:T(8,128)}, s32[]{:T(128)}, f32[256,16]{0,1:T(8,128)S(1)}, /*index=5*/bf1...) while((s32[]{:T(128)}, f32[16,128,128]{2,1,0:T(8,128)S(1)}, ...), condition=%wide.region_15.16_spmd, body=%wide.region_13.15_spmd.sunk | while | flops 1446003712 | bytes 21269528 | solution.py:166
  794.2 2.4 fusion.466
  796.7 2.2 convolution_add_fusion.19
  811.9 2.4 fusion.466
  814.4 2.2 convolution_add_fusion.19
  829.6 2.4 fusion.466
  832.0 2.2 convolution_add_fusion.19
  847.2 2.4 fusion.466
  849.7 2.2 convolution_add_fusion.19
  851.9 2.2 multiply_reduce_fusion.1
  (1269 shorter events, 522.0 us)
Async XLA Ops:
  7.2 372.3 %copy-start = (bf16[1,1,256,2048]{3,2,1,0:T(8,128)(2,1)S(1)}, bf16[1,1,256,2048]{3,2,1,0:T(8,128)(2,1)}, u32[]{:S(2)}) copy-start(bf16[1,1,256,2048]{3,2,1,0:T(8,128)(2,1)} %param.20) | copy-start | bytes 3145732
  7.2 71.0 %all-gather.12.cloned.1.call-start = ((), (), s32[]{:S(2)}) async-start(), calls=%async_computation | async-start | bytes 2228224 | tf_op jit(solution)/shard_map/all_gather | solution.py:202
  7.9 96.5 %all-gather.14.cloned.1.call-start = ((), (), s32[]{:S(2)}) async-start(), calls=%async_computation.1 | async-start | bytes 4456448 | tf_op jit(solution)/shard_map/all_gather | solution.py:203
  8.7 371.6 %all-gather.16.cloned.1.call-start = ((), (), s32[]{:S(2)}) async-start(), calls=%async_computation.2 | async-start | bytes 2228224 | tf_op jit(solution)/shard_map/all_gather | solution.py:201
  9.4 379.2 %all-gather.20.cloned.1.call-start = ((), (), s32[]{:S(2)}) async-start(), calls=%async_computation.4 | async-start | bytes 4456448 | tf_op jit(solution)/shard_map/all_gather | solution.py:219
  17.0 40.0 %copy-start.11 = (bf16[128,8]{0,1:T(8,128)(2,1)S(1)}, bf16[128,8]{0,1:T(8,128)(2,1)}, u32[]{:S(2)}) copy-start(bf16[128,8]{0,1:T(8,128)(2,1)} %param.25) | copy-start | bytes 6148
  17.0 57.5 %copy-start.13 = (f32[16]{0:T(128)S(1)}, f32[16]{0:T(128)}, u32[]{:S(2)}) copy-start(f32[16]{0:T(128)} %param.27) | copy-start | bytes 196
  17.0 384.6 %all-gather.24.cloned.1.call-start = ((), (), s32[]{:S(2)}) async-start(), calls=%async_computation.6 | async-start | bytes 4456448 | tf_op jit(solution)/shard_map/all_gather | solution.py:218
  23.1 391.5 %all-gather.22.cloned.1.call-start = ((), (), s32[]{:S(2)}) async-start(), calls=%async_computation.5 | async-start | bytes 8912896 | tf_op jit(solution)/shard_map/all_gather | solution.py:220
  32.2 400.7 %all-gather.26.cloned.1.call-start = ((), (), s32[]{:S(2)}) async-start(), calls=%async_computation.7 | async-start | bytes 8912896 | tf_op jit(solution)/shard_map/all_gather | solution.py:231
  115.0 220.6 %copy-start.14 = (f32[16]{0:T(128)S(1)}, f32[16]{0:T(128)}, u32[]{:S(2)}) copy-start(f32[16]{0:T(128)} %param.26) | copy-start | bytes 196
  115.0 220.6 %copy-start.10 = (bf16[128,8]{0,1:T(8,128)(2,1)S(1)}, bf16[128,8]{0,1:T(8,128)(2,1)}, u32[]{:S(2)}) copy-start(bf16[128,8]{0,1:T(8,128)(2,1)} %param.24) | copy-start | bytes 6148
  115.0 264.4 %copy-start.12 = (f32[128]{0:T(128)S(1)}, f32[128]{0:T(128)}, u32[]{:S(2)}) copy-start(f32[128]{0:T(128)} %param.28) | copy-start | bytes 1540
  333.2 0.8 copy-start.4
  333.2 1.0 copy-start.3
  334.1 149.1 %all-gather.28.cloned.1.call-start = ((), (), s32[]{:S(2)}) async-start(), calls=%async_computation.8 | async-start | bytes 8912896 | tf_op jit(solution)/shard_map/all_gather | solution.py:232
  334.8 443.4 %all-gather.18.cloned.1.call-start = ((), (), s32[]{:S(2)}) async-start(), calls=%async_computation.3 | async-start | bytes 1572864 | tf_op jit(solution)/shard_map/all_gather | solution.py:246
  527.4 0.8 copy-start.5
  764.4 7.6 copy-start.7
  773.4 2.2 copy-start.6
  775.6 2.7 copy-start.8
  775.6 2.9 copy-start.9
  778.3 3.0 copy-start.2
  854.1 4.4 copy-start.1
Sparse Core Ops, SparseCore 0:
  10.2 41.7 all-gather.11
  54.1 50.2 all-gather.13
  106.6 38.9 all-gather.15
  147.6 50.4 all-gather.19
  200.1 49.2 all-gather.23
  251.4 72.9 all-gather.21
  334.2 73.5 all-gather.25
  409.9 73.2 all-gather.27
  528.4 20.1 all-gather.17
where the time goes:
time: 880 us; the launch traced here: 865 us
  matrix products  497 us (56%)
  blocking collectives  103 us (12%)
  local copies, waits for them, and re-layouts  97.2 us (11%)
  other arithmetic  75.7 us (9%)
  waiting for transfers between devices  69.5 us (8%)
  between operations  15.4 us (2%)
    dot_general x180, matrix products, invert_unit(): jnp.einsum('hij,hjl->hil', inverse, ident + power, precision=highest_level)  75.7 us
    dot_general x36, matrix products, span_core(): jnp.einsum('cwx,cwq->wxq', tail_tokens, delta_update, precision=highest_l...  74.9 us
    dot_general x180, matrix products, invert_unit(): power = jnp.einsum('hij,hjl->hil', power, power, precision=highest_level)  74.3 us
    all_gather x1, waiting for transfers between devices, shards(): lax.all_gather(local_end[None], 'seq', axis=0, tiled=True)  50.3 us
    mul x36, other arithmetic, span_core(): (beta * decay_factor)[..., None] * key_float  43.2 us
    dot_general x36, matrix products, span_core(): jnp.einsum('ihk,jhk->hij', keys, keys, preferred_element_type=jnp.float32)  40.2 us
    dot_general x10, matrix products, adder(): jnp.dot(left, p, preferred_element_type=jnp.float32)  39 us
    dot_general x16, matrix products, span_core(): jnp.einsum('ihk,ihj->hkj', tail_tokens, key_weights, precision=highest_le...  32.2 us
  transfers between devices with their start and end apart: 9, of which 2 were waited for; matrix products, arithmetic and copies ran while one was open for 63% of the time, Pallas kernels for 0%

commit v1 on v0

v1 whole, which is shorter than its diff:
```python
import functools

import jax
import jax.numpy as jnp
from jax import lax
from jax.experimental import pallas as pl
from jax.experimental.pallas import tpu as pltpu
from jax.sharding import PartitionSpec as P

DK = 128
CHUNK = 128
ROWS = 256
LANES = 128
BF = jnp.bfloat16
F32 = jnp.float32


def dot(a, b):
    return jnp.dot(a, b, preferred_element_type=F32)


def dot_nt(a, b):
    return lax.dot_general(a, b, (((1,), (1,)), ((), ())), preferred_element_type=F32)


def block_kernel(
    key_heads, value_heads, span, x_ref, w_ref, rate_ref, shift_ref,
    out_ref, lift_ref, map_ref, raw, carry,
):
    repeat = value_heads // key_heads
    step = pl.program_id(0)
    heads = range(value_heads)
    row = lax.broadcasted_iota(jnp.int32, (CHUNK, CHUNK), 0)
    col = lax.broadcasted_iota(jnp.int32, (CHUNK, CHUNK), 1)
    ident = jnp.where(row == col, 1.0, 0.0).astype(F32)

    @pl.when(lax.rem(step, span) == 0)
    def _():
        for h in heads:
            carry[h, :, :DK] = ident
            carry[h, :, DK:] = jnp.zeros((DK, DK), F32)

    x = x_ref[...]
    total = w_ref.shape[1]
    for at in range(0, total, 512):
        size = min(512, total - at)
        raw[:, at:at + size] = dot(x, w_ref[:, at:at + size])

    @pl.loop(0, ROWS // CHUNK)
    def _(c):
        rows = pl.ds(pl.multiple_of(c * CHUNK, CHUNK), CHUNK)
        within = row >= col
        differ = row ^ col
        gates = raw[rows, total - LANES:]
        log_decay = -rate_ref[...] * jax.nn.softplus(gates)
        beta = jax.nn.sigmoid(gates + shift_ref[...])
        lower_ones = jnp.where(within, 1.0, 0.0).astype(F32)
        cumul = jnp.dot(
            lower_ones, log_decay, preferred_element_type=F32, precision=lax.Precision.HIGHEST
        )
        cumul_t = cumul.T
        beta_t = beta.T
        factor = jnp.exp(cumul)
        factor_t = jnp.exp(cumul_t)
        tail_t = jnp.exp(cumul_t[:, CHUNK - 1:] - cumul_t)
        masks = []
        size = 2
        while size < CHUNK:
            masks.append(
                jnp.where((differ >= size) & (differ < 2 * size) & within, 1.0, 0.0).astype(BF)
            )
            size *= 2

        queries, keys, keys_t, dots = [], [], [], []
        for j in range(key_heads):
            q = raw[rows, j * DK:(j + 1) * DK]
            k = raw[rows, (key_heads + j) * DK:(key_heads + j + 1) * DK]
            q = q * lax.rsqrt(jnp.sum(q * q, axis=-1, keepdims=True) + 1e-06) * DK ** (-0.5)
            k = k * lax.rsqrt(jnp.sum(k * k, axis=-1, keepdims=True) + 1e-06)
            q, k = q.astype(BF), k.astype(BF)
            queries.append(q.astype(F32))
            keys.append(k)
            keys_t.append(k.astype(F32).T)
            dots.append(dot_nt(jnp.concatenate([q, k], axis=0), k))

        lowers, inverses, scores = [], [], []
        for h in heads:
            both = dots[h // repeat]
            spread = cumul[:, h:h + 1] - cumul_t[h:h + 1, :]
            decay = jnp.where(within, jnp.exp(spread), 0.0)
            scores.append((decay * both[:CHUNK]).astype(BF))
            lower = jnp.where(
                differ > 0,
                beta[:, value_heads + h:value_heads + h + 1] * decay * both[CHUNK:],
                0.0,
            )
            inverses.append(ident - jnp.where(differ == 1, lower, 0.0))
            lowers.append(lower.astype(BF))
        for mask in masks:
            small = [x.astype(BF) for x in inverses]
            mids = [dot(lowers[h] * mask, small[h]).astype(BF) for h in heads]
            inverses = [inverses[h] - dot(small[h], mids[h]) for h in heads]

        solved = []
        for h in heads:
            b_row = beta_t[value_heads + h:value_heads + h + 1, :]
            scaled = inverses[h] * b_row
            at = (2 * key_heads + h) * DK
            values = raw[rows, at:at + DK].astype(BF)
            fresh = dot(scaled.astype(BF), values)
            weights = dot((scaled * factor_t[h:h + 1, :]).astype(BF), keys[h // repeat])
            solved.append(jnp.concatenate([weights, fresh], axis=1).astype(BF))
        parts = []
        for h in heads:
            tails = (keys_t[h // repeat] * tail_t[h:h + 1, :]).astype(BF)
            parts.append(dot(jnp.concatenate([scores[h], tails], axis=0), solved[h]))
        for h in heads:
            part = parts[h]
            lifted = factor[:, h:h + 1] * queries[h // repeat] - part[:CHUNK, :DK]
            state = carry[h]
            left = jnp.concatenate([lifted, -part[CHUNK:, :DK]], axis=0).astype(BF)
            moved = dot(left, state.astype(BF))
            last = factor[CHUNK - 1:, h:h + 1]
            span_cols = slice(h * DK, (h + 1) * DK)
            out_ref[rows, span_cols] = moved[:CHUNK, DK:] + part[:CHUNK, DK:]
            lift_ref[rows, span_cols] = moved[:CHUNK, :DK].astype(BF)
            fresh_state = last * state + moved[CHUNK:]
            carry[h, :, :DK] = fresh_state[:, :DK]
            carry[h, :, DK:] = fresh_state[:, DK:] + part[CHUNK:, DK:]

    @pl.when(step == pl.num_programs(0) - 1)
    def _():
        for h in heads:
            map_ref[h, :, :DK] = (carry[h, :, :DK] - ident).astype(BF)
            map_ref[h, :, DK:] = carry[h, :, DK:].astype(BF)


def run_blocks(x, weights, rate, shift, key_heads, value_heads, span):
    count, depth = x.shape
    total = weights.shape[1]
    width = value_heads * DK
    whole = lambda shape: pl.BlockSpec(shape, lambda i: (0,) * len(shape))
    return pl.pallas_call(
        functools.partial(block_kernel, key_heads, value_heads, span),
        grid=(count // ROWS,),
        in_specs=[
            pl.BlockSpec((ROWS, depth), lambda i: (i, 0)),
            pl.BlockSpec((depth, total), lambda i: (0, 0), pipeline_mode=pl.Buffered(1)),
            whole((1, LANES)),
            whole((1, LANES)),
        ],
        out_specs=[
            pl.BlockSpec((ROWS, width), lambda i: (i, 0)),
            pl.BlockSpec((ROWS, width), lambda i: (i, 0)),
            whole((value_heads, DK, 2 * DK)),
        ],
        out_shape=[
            jax.ShapeDtypeStruct((count, width), F32),
            jax.ShapeDtypeStruct((count, width), BF),
            jax.ShapeDtypeStruct((value_heads, DK, 2 * DK), BF),
        ],
        scratch_shapes=[
            pltpu.VMEM((ROWS, total), F32),
            pltpu.VMEM((value_heads, DK, 2 * DK), F32),
        ],
        compiler_params=pltpu.CompilerParams(
            dimension_semantics=("arbitrary",), vmem_limit_bytes=48 * 1024 * 1024
        ),
        cost_estimate=pl.CostEstimate(
            flops=2 * count * depth * total + 2 * count * width * 2600,
            bytes_accessed=2 * count * depth + 2 * depth * total + 6 * count * width,
            transcendentals=count * value_heads * DK,
        ),
    )(x, weights, rate, shift)


def scan_kernel(me_ref, maps_ref, start_ref, end_ref, state):
    step = pl.program_id(0)
    heads = range(state.shape[0])

    @pl.when(step == 0)
    def _():
        state[...] = jnp.zeros_like(state)

    @pl.when(step == me_ref[0])
    def _():
        start_ref[...] = state[...].astype(BF)

    for h in heads:
        held = state[h]
        high = held.astype(BF)
        low = (held - high.astype(F32)).astype(BF)
        moved = dot(maps_ref[0, h, :, :DK], jnp.concatenate([high, low], axis=1))
        state[h] = held + (moved[:, :DK] + moved[:, DK:]) + maps_ref[0, h, :, DK:].astype(F32)

    @pl.when(step == pl.num_programs(0) - 1)
    def _():
        end_ref[...] = state[...].astype(BF)


def run_scan(me, maps):
    count, heads = maps.shape[:2]
    one = pl.BlockSpec((heads, DK, DK), lambda i: (0, 0, 0))
    shape = jax.ShapeDtypeStruct((heads, DK, DK), BF)
    return pl.pallas_call(
        scan_kernel,
        grid=(count,),
        in_specs=[
            pl.BlockSpec(memory_space=pltpu.SMEM),
            pl.BlockSpec((1,) + maps.shape[1:], lambda i: (i, 0, 0, 0)),
        ],
        out_specs=[one, one],
        out_shape=[shape, shape],
        scratch_shapes=[pltpu.VMEM((heads, DK, DK), F32)],
        compiler_params=pltpu.CompilerParams(
            dimension_semantics=("arbitrary",), vmem_limit_bytes=32 * 1024 * 1024
        ),
    )(me, maps)


def finish_kernel(out_ref, lift_ref, state_ref, gain_ref, done_ref):
    for h in range(state_ref.shape[0]):
        cols = slice(h * DK, (h + 1) * DK)
        o = out_ref[:, cols] + dot(lift_ref[:, cols], state_ref[h])
        mean = jnp.mean(o * o, axis=-1, keepdims=True)
        done_ref[:, cols] = (o * lax.rsqrt(mean + 1e-06) * gain_ref[...]).astype(BF)


def run_finish(out, lifted, state, gain):
    count, width = out.shape
    rows = pl.BlockSpec((ROWS, width), lambda i: (i, 0))
    return pl.pallas_call(
        finish_kernel,
        grid=(count // ROWS,),
        in_specs=[
            rows,
            rows,
            pl.BlockSpec(state.shape, lambda i: (0, 0, 0)),
            pl.BlockSpec((1, DK), lambda i: (0, 0)),
        ],
        out_specs=rows,
        out_shape=jax.ShapeDtypeStruct((count, width), BF),
        compiler_params=pltpu.CompilerParams(
            dimension_semantics=("arbitrary",), vmem_limit_bytes=32 * 1024 * 1024
        ),
        cost_estimate=pl.CostEstimate(
            flops=2 * count * width * DK, bytes_accessed=8 * count * width, transcendentals=0
        ),
    )(out, lifted, state, gain)


def shards(
    n_grp,
    prompt_tokens,
    response_tokens,
    w_query,
    w_key,
    w_value,
    w_decay,
    w_beta,
    decay_rate,
    beta_shift,
    out_gain,
    resp_lengths,
):
    value_heads = w_decay.shape[1]
    key_heads = w_key.shape[1] // DK
    grp = lax.axis_index("grp")
    pad = LANES - 2 * value_heads
    first_head = grp * value_heads
    rate = lax.dynamic_slice_in_dim(decay_rate, first_head, value_heads)
    shift = lax.dynamic_slice_in_dim(beta_shift, first_head, value_heads)
    rate = jnp.pad(rate, (0, LANES - value_heads)).reshape(1, LANES)
    shift = jnp.pad(shift, (value_heads, pad)).reshape(1, LANES)
    gain = out_gain.reshape(1, DK)
    columns = jnp.concatenate(
        [w_query, w_key, w_value, w_decay, w_beta, jnp.zeros((w_decay.shape[0], pad), BF)], axis=1
    )
    weights = lax.all_gather(columns, "seq", axis=0, tiled=True)
    length, depth = response_tokens.shape[2:]
    tokens = lax.all_gather(response_tokens.reshape(length, depth), "grp", axis=0, tiled=True)

    blocks = prompt_tokens.shape[0] // ROWS
    out, lifted, own_map = run_blocks(
        prompt_tokens, weights, rate, shift, key_heads, value_heads, blocks
    )
    maps = lax.all_gather(own_map[None], "seq", axis=0, tiled=True)
    r_out, r_lifted, _ = run_blocks(
        tokens, weights, rate, shift, key_heads, value_heads, length // ROWS
    )
    start, end = run_scan(lax.axis_index("seq").reshape(1), maps)
    r_done = run_finish(r_out, r_lifted, end, gain).reshape(n_grp, length, -1)
    prompt_output = run_finish(out, lifted, start, gain)
    exchanged = lax.all_to_all(r_done, "grp", split_axis=0, concat_axis=0, tiled=True)
    finished = jnp.swapaxes(exchanged, 0, 1).reshape(length, -1)
    positions = lax.broadcasted_iota(jnp.int32, (length, 1), 0)
    masked = jnp.where(positions < resp_lengths.reshape(()), finished, jnp.zeros_like(finished))
    return (prompt_output, masked.reshape(1, 1, length, masked.shape[1]))


def solution(mesh):
    placed = (
        P("seq", None),
        P("grp", "seq", None, None),
        P("seq", "grp"),
        P("seq", "grp"),
        P("seq", "grp"),
        P("seq", "grp"),
        P("seq", "grp"),
        P(),
        P(),
        P(),
        P("grp", "seq"),
    )
    return jax.shard_map(
        functools.partial(shards, mesh.shape["grp"]),
        mesh=mesh,
        in_specs=placed,
        out_specs=(P("seq", "grp"), P("grp", "seq", None, None)),
        check_vma=False,
    )
```

time: 880 us -> 246 us (0.28); the launches traced: 865 us -> 243 us
  matrix products: 497 us -> 0 us
  blocking collectives: 103 us -> 0 us
  local copies, waits for them, and re-layouts: 97.2 us -> 15.4 us
  Pallas kernels: 0 us -> 75.6 us
  other arithmetic: 75.7 us -> 1.12 us
  waiting for transfers between devices: 69.5 us -> 133 us
    dot_general x622 -> x0, matrix products: 497 us -> none  [the longest x180 75.7 us: invert_unit(): jnp.einsum('hij,hjl->hil', inverse, ident + power, precision=highest_level)]
    all_gather x9 -> x0, blocking collectives: 103 us -> none  [the longest x1 19.6 us: shards(): lax.all_gather(weights[3], 'seq', axis=0, tiled=True)]
    pallas_call x0 -> x5, Pallas kernels: none -> 75.6 us  [the longest x2 65.5 us: run_blocks(): pl.pallas_call(functools.partial(block_kernel, key_heads, value_heads, sp...]
    all_gather x9 -> x3, waiting for transfers between devices: 66.7 us -> 124 us  [the longest x1 76.4 us: shards(): weights = lax.all_gather(columns, 'seq', axis=0, tiled=True)]
    mul x68 -> x0, other arithmetic: 43.8 us -> none  [the longest x36 43.2 us: span_core(): (beta * decay_factor)[..., None] * key_float]
    dot_general x3 -> x0, local copies, waits for them, and re-layouts: 25.5 us -> none  [adder(): jnp.dot(left, p, preferred_element_type=jnp.float32)]
    squeeze x33 -> x0, local copies, waits for them, and re-layouts: 25.5 us -> none  [the longest x32 24.4 us: block_pass(): lax.scan(block_advance, (state_matrix, ident), pieces)]
    dynamic_update_slice x16 -> x0, other arithmetic: 13.6 us -> none  [shards(): end, starts = lax.scan(body_advance, zero_state, (all_maps, all_ends))]
  transfers between devices with their start and end apart: 9 -> 4, of which waited for: 2 -> 3; matrix products, arithmetic and copies ran while one was open for 63% -> 1% of each run, Pallas kernels for 0% -> 28%
where the time goes in v1:
time: 246 us; the launch traced here: 243 us
  waiting for transfers between devices  133 us (54%)
  Pallas kernels  75.6 us (31%)
  local copies, waits for them, and re-layouts  15.4 us (6%)
  between operations  14.5 us (6%)
  starting transfers between devices  3.7 us (2%)
    all_gather x1, waiting for transfers between devices, shards(): weights = lax.all_gather(columns, 'seq', axis=0, tiled=True)  76.4 us
    pallas_call x2, Pallas kernels, run_blocks(): pl.pallas_call(functools.partial(block_kernel, key_heads, value_heads, sp...  65.5 us
    all_gather x1, waiting for transfers between devices, shards(): maps = lax.all_gather(own_map[None], 'seq', axis=0, tiled=True)  47.4 us
    unnamed x14, local copies, waits for them, and re-layouts  10.1 us
    all_to_all x1, waiting for transfers between devices, shards(): lax.all_to_all(r_done, 'grp', split_axis=0, concat_axis=0, tiled=True)  8.3 us
    pallas_call x1, Pallas kernels, run_scan(): pl.pallas_call(scan_kernel, grid=(count,), in_specs=[pl.BlockSpec(memory_...  5.08 us
    pallas_call x2, Pallas kernels, run_finish(): pl.pallas_call(finish_kernel, grid=(count // ROWS,), in_specs=[rows, rows...  5.02 us
  transfers between devices with their start and end apart: 4, of which 3 were waited for; matrix products, arithmetic and copies ran while one was open for 1% of the time, Pallas kernels for 28%

profile of v1, /device:TPU:8, one launch (start us, length us, event | category | flops | bytes accessed | tf_op | source)
XLA Modules:
  0.0 243.2 jit_solution(4623204305945584455)
XLA Ops:
  7.2 0.0 all-gather.6.cloned.1.call-start
  7.2 0.8 copy.16
  8.0 0.8 copy.17
  8.8 1.9 concatenate.3
  10.7 0.0 all-gather.6.cloned.1.call-update
  10.8 0.0 all-gather.10.cloned.1.call-start
  10.8 0.7 all-gather.10.cloned.1.call-update
  11.5 0.0 all-gather.8.cloned.1.call-start
  11.6 0.7 dynamic_slice.6
  12.3 0.7 dynamic_slice.7
  13.0 0.1 pad_bitcast_fusion
  13.1 76.4 %all-gather.6.cloned.1.call-done.w_ref = bf16[2048,2176]{1,0:T(8,128)(2,1)} async-done(((bf16[128,2176]{1,0:T(8,128)(2,1)}), bf16[2048,2176]{1,0:T(8,128)(2,1)}) %all-gather.6.cloned.1.call-update) | async-done | bytes 8912912 | tf_op jit(solution)/shard_map/all_gather | solution.py:279
  89.5 42.4 %shard_map.122 = (f32[1024,1024]{1,0:T(8,128)}, bf16[1024,1024]{1,0:T(8,128)(2,1)S(1)}, bf16[8,128,256]{2,1,0:T(8,128)(2,1)}) custom-call(bf16[1024,2048]{1,0:T(8,128)(2,1)} %x_ref.1, bf16[2048,2176]{1,0:T(8,128)(2,1)} %all-gather.6.cloned.1.call-done.w_ref, f32[1,128]{1,0:T(1,128)S(1)} %get-tuple-element.17.rate_ref, f32[1,128]{1,0:T(1,128)S(1)} %get-tuple-element.16.shift_ref), custom_call_target="tpu_custom_call" | custom-call | flops 14579400704 | bytes 19398656 | tf_op jit(solution)/shard_map/pallas_call | solution.py:143
  131.9 0.0 all-gather.8.cloned.1.call-update
  132.0 0.0 all-gather.10.cloned.1.call-done
  132.0 0.0 copy-start.5
  132.0 1.6 copy-done.5
  133.6 23.0 %shard_map.125 = (f32[512,1024]{1,0:T(8,128)S(1)}, bf16[512,1024]{1,0:T(8,128)(2,1)S(1)}, bf16[8,128,256]{2,1,0:T(8,128)(2,1)}) custom-call(bf16[512,2048]{1,0:T(8,128)(2,1)S(1)} %bitcast.15, bf16[2048,2176]{1,0:T(8,128)(2,1)} %all-gather.6.cloned.1.call-done.w_ref, f32[1,128]{1,0:T(1,128)S(1)} %get-tuple-element.17.rate_ref, ...), custom_call_target="tpu_custom_call" | custom-call | flops 7289700352 | bytes 14155776 | tf_op jit(solution)/shard_map/pallas_call | solution.py:143
  156.6 0.0 copy-start.2
  156.6 1.3 copy-done.2
  157.9 47.4 %all-gather.8.cloned.1.call-done = bf16[128,128,256]{2,1,0:T(8,128)(2,1)} async-done(((bf16[8,128,256]{2,1,0:T(8,128)(2,1)}), bf16[128,128,256]{2,1,0:T(8,128)(2,1)}) %all-gather.8.cloned.1.call-update) | async-done | bytes 8388624 | tf_op jit(solution)/shard_map/all_gather | solution.py:287
  205.4 0.0 copy-start
  205.4 3.4 %copy-done = bf16[128,128,256]{2,1,0:T(8,128)(2,1)S(1)} copy-done((bf16[128,128,256]{2,1,0:T(8,128)(2,1)S(1)}, bf16[128,128,256]{2,1,0:T(8,128)(2,1)}, u32[]{:S(2)}) %copy-start) | copy-done | bytes 8388632
  208.7 0.0 copy-start.3
  208.7 0.0 copy-start.4
  208.7 5.1 %shard_map.123 = (bf16[8,128,128]{2,1,0:T(8,128)(2,1)S(1)}, bf16[8,128,128]{2,1,0:T(8,128)(2,1)S(1)}) custom-call(s32[1]{0:T(128)} %bitcast.2.me_ref, bf16[16,8,128,256]{3,2,1,0:T(8,128)(2,1)S(1)} %bitcast.12), custom_call_target="tpu_custom_call" | custom-call | tf_op jit(solution)/shard_map/pallas_call | solution.py:205
  213.8 0.0 copy-done.3
  213.8 0.0 copy-done.4
  213.8 1.9 shard_map.126
  215.7 3.6 %all-to-all-start = ((bf16[2,256,1024]{2,1,0:T(8,128)(2,1)}), bf16[2,256,1024]{2,1,0:T(8,128)(2,1)S(1)}, u32[]{:S(2)}, u32[]{:S(2)}) async-start(bf16[2,256,1024]{2,1,0:T(8,128)(2,1)} %bitcast.7), calls=%async_computation | async-start | bytes 2097152 | tf_op jit(solution)/shard_map/all_to_all | solution.py:294
  220.0 0.0 copy-start.1
  220.0 2.2 copy-done.1
  222.2 3.1 %shard_map.124 = bf16[1024,1024]{1,0:T(8,128)(2,1)} custom-call(f32[1024,1024]{1,0:T(8,128)S(1)} %copy-done.1, bf16[1024,1024]{1,0:T(8,128)(2,1)S(1)} %get-tuple-element.10.lift_ref, bf16[8,128,128]{2,1,0:T(8,128)(2,1)S(1)} %get-tuple-element.12.state_ref, f32[1,128]{1,0:T(1,128)S(1)} %bitcast.14), custom_call_target="tpu_custom_call" | custom-call | flops 268435456 | bytes 8388608 | tf_op jit(solution)/shard_map/pallas_call | solution.py:232
  225.3 8.3 %all-to-all-done = bf16[2,256,1024]{2,1,0:T(8,128)(2,1)S(1)} async-done(((bf16[2,256,1024]{2,1,0:T(8,128)(2,1)}), bf16[2,256,1024]{2,1,0:T(8,128)(2,1)S(1)}, u32[]{:S(2)}, u32[]{:S(2)}) %all-to-all-start) | async-done | bytes 1048608 | tf_op jit(solution)/shard_map/all_to_all | solution.py:294
  233.6 1.1 copy.18
  234.7 0.8 reshape.70
  235.5 1.1 broadcast_select_fusion
  (2 shorter events, 0.0 us)
Async XLA Ops:
  7.2 82.3 %all-gather.6.cloned.1.call-start = ((), (), s32[]{:S(2)}) async-start(), calls=%async_computation.1 | async-start | bytes 9469952 | tf_op jit(solution)/shard_map/all_gather | solution.py:279
  10.8 121.2 %all-gather.10.cloned.1.call-start = ((), (), s32[]{:S(2)}) async-start(), calls=%async_computation.3 | async-start | bytes 3145728 | tf_op jit(solution)/shard_map/all_gather | solution.py:281
  11.5 193.8 %all-gather.8.cloned.1.call-start = ((), (), s32[]{:S(2)}) async-start(), calls=%async_computation.2 | async-start | bytes 8912896 | tf_op jit(solution)/shard_map/all_gather | solution.py:287
  132.0 1.6 copy-start.5
  156.6 1.3 copy-start.2
  205.4 3.4 %copy-start = (bf16[128,128,256]{2,1,0:T(8,128)(2,1)S(1)}, bf16[128,128,256]{2,1,0:T(8,128)(2,1)}, u32[]{:S(2)}) copy-start(bf16[128,128,256]{2,1,0:T(8,128)(2,1)} %all-gather.8.cloned.1.call-done) | copy-start | bytes 25165828
  208.7 5.1 %copy-start.3 = (f32[512,1024]{1,0:T(8,128)S(1)}, f32[512,1024]{1,0:T(8,128)}, u32[]{:S(2)}) copy-start(f32[512,1024]{1,0:T(8,128)} %copy-done.2) | copy-start | bytes 6291460
  208.7 5.1 %copy-start.4 = (f32[128]{0:T(128)S(1)}, f32[128]{0:T(128)}, u32[]{:S(2)}) copy-start(f32[128]{0:T(128)} %param.20) | copy-start | bytes 1540
  215.7 17.9 %all-to-all-start = ((bf16[2,256,1024]{2,1,0:T(8,128)(2,1)}), bf16[2,256,1024]{2,1,0:T(8,128)(2,1)S(1)}, u32[]{:S(2)}, u32[]{:S(2)}) async-start(bf16[2,256,1024]{2,1,0:T(8,128)(2,1)} %bitcast.7), calls=%async_computation | async-start | bytes 2097152 | tf_op jit(solution)/shard_map/all_to_all | solution.py:294
  220.0 2.2 copy-start.1
Sparse Core Ops, SparseCore 0:
  10.9 78.5 all-gather.5
  91.0 32.0 all-gather.9
  132.1 73.2 all-gather.7

commit v2 on v1

--- a/solution.py
+++ b/solution.py
@@ -130,15 +130,21 @@
 
     @pl.when(step == pl.num_programs(0) - 1)
     def _():
-        for h in heads:
-            map_ref[h, :, :DK] = (carry[h, :, :DK] - ident).astype(BF)
-            map_ref[h, :, DK:] = carry[h, :, DK:].astype(BF)
-
-
-def run_blocks(x, weights, rate, shift, key_heads, value_heads, span):
+        parts = map_ref.shape[0] // value_heads
+        width = DK // parts
+        for h in heads:
+            moves = (carry[h, :, :DK] - ident).astype(BF)
+            ends = carry[h, :, DK:].T.astype(BF)
+            for p in range(parts):
+                map_ref[h * parts + p, :DK] = moves
+                map_ref[h * parts + p, DK:] = ends[p * width:(p + 1) * width]
+
+
+def run_blocks(x, weights, rate, shift, key_heads, value_heads, span, takers):
     count, depth = x.shape
     total = weights.shape[1]
     width = value_heads * DK
+    map_rows = DK + DK * value_heads // takers
     whole = lambda shape: pl.BlockSpec(shape, lambda i: (0,) * len(shape))
     return pl.pallas_call(
         functools.partial(block_kernel, key_heads, value_heads, span),
@@ -152,12 +158,12 @@
         out_specs=[
             pl.BlockSpec((ROWS, width), lambda i: (i, 0)),
             pl.BlockSpec((ROWS, width), lambda i: (i, 0)),
-            whole((value_heads, DK, 2 * DK)),
+            whole((takers, map_rows, DK)),
         ],
         out_shape=[
             jax.ShapeDtypeStruct((count, width), F32),
             jax.ShapeDtypeStruct((count, width), BF),
-            jax.ShapeDtypeStruct((value_heads, DK, 2 * DK), BF),
+            jax.ShapeDtypeStruct((takers, map_rows, DK), BF),
         ],
         scratch_shapes=[
             pltpu.VMEM((ROWS, total), F32),
@@ -174,54 +180,179 @@
     )(x, weights, rate, shift)
 
 
-def scan_kernel(me_ref, maps_ref, start_ref, end_ref, state):
-    step = pl.program_id(0)
-    heads = range(state.shape[0])
-
-    @pl.when(step == 0)
-    def _():
-        state[...] = jnp.zeros_like(state)
-
-    @pl.when(step == me_ref[0])
-    def _():
-        start_ref[...] = state[...].astype(BF)
-
-    for h in heads:
-        held = state[h]
-        high = held.astype(BF)
-        low = (held - high.astype(F32)).astype(BF)
-        moved = dot(maps_ref[0, h, :, :DK], jnp.concatenate([high, low], axis=1))
-        state[h] = held + (moved[:, :DK] + moved[:, DK:]) + maps_ref[0, h, :, DK:].astype(F32)
-
-    @pl.when(step == pl.num_programs(0) - 1)
-    def _():
-        end_ref[...] = state[...].astype(BF)
-
-
-def run_scan(me, maps):
-    count, heads = maps.shape[:2]
-    one = pl.BlockSpec((heads, DK, DK), lambda i: (0, 0, 0))
-    shape = jax.ShapeDtypeStruct((heads, DK, DK), BF)
+def scan_kernel(maps_ref, states_ref):
+    count, rows = maps_ref.shape[:2]
+    held = jnp.zeros((rows - DK, DK), F32)
+    for i in range(count):
+        states_ref[i, 0] = held.astype(BF)
+        high = held.astype(BF).astype(F32)
+        both = jnp.concatenate([high, held - high], axis=0).astype(BF)
+        moved = dot_nt(both, maps_ref[i, :DK])
+        held = held + (moved[:rows - DK] + moved[rows - DK:]) + maps_ref[i, DK:].astype(F32)
+    for i in range(count):
+        states_ref[i, 1] = held.astype(BF)
+
+
+def run_scan(maps):
+    count, rows = maps.shape[:2]
     return pl.pallas_call(
         scan_kernel,
-        grid=(count,),
-        in_specs=[
-            pl.BlockSpec(memory_space=pltpu.SMEM),
-            pl.BlockSpec((1,) + maps.shape[1:], lambda i: (i, 0, 0, 0)),
-        ],
-        out_specs=[one, one],
-        out_shape=[shape, shape],
-        scratch_shapes=[pltpu.VMEM((heads, DK, DK), F32)],
-        compiler_params=pltpu.CompilerParams(
-            dimension_semantics=("arbitrary",), vmem_limit_bytes=32 * 1024 * 1024
+        out_shape=jax.ShapeDtypeStruct((count, 2, rows - DK, DK), BF),
+        in_specs=[pl.BlockSpec(memory_space=pltpu.VMEM)],
+        out_specs=pl.BlockSpec(memory_space=pltpu.VMEM),
+        compiler_params=pltpu.CompilerParams(vmem_limit_bytes=16 * 1024 * 1024),
+    )(maps)
+
+
+def gather_kernel(count, own_ref, all_ref, own_sem, send_sems, recv_sems):
+    size = own_ref.shape[0]
+    me = lax.axis_index("seq")
+    grp = lax.axis_index("grp")
+    depth = count // 4
+    z, place = lax.div(me, 4), lax.rem(me, 4)
+    y, core = lax.div(place, 2), lax.rem(place, 2)
+    across = z * 4 + (1 - y) * 2 + core
+    twin = z * 4 + y * 2 + (1 - core)
+    above, below = me + 4, me - 4
+
+    def rows(block):
+        return pl.ds(pl.multiple_of(block * size, size), size)
+
+    def copy(block, way, target, source=None):
+        return pltpu.make_async_remote_copy(
+            src_ref=all_ref.at[rows(block)] if source is None else source,
+            dst_ref=all_ref.at[rows(block)],
+            send_sem=send_sems.at[block, way],
+            recv_sem=recv_sems.at[block],
+            device_id=(target, grp),
+            device_id_type=pl.DeviceIdType.MESH,
+        )
+
+    def arrived(block):
+        copy(block, 3, twin).wait_recv()
+
+    barrier = pltpu.get_barrier_semaphore()
+
+    def greet(target):
+        pl.semaphore_signal(
+            barrier, inc=1, device_id=(target, grp), device_id_type=pl.DeviceIdType.MESH
+        )
+
+    greet(across)
+    greet(twin)
+
+    @pl.when(z < depth - 1)
+    def _():
+        greet(above)
+
+    @pl.when(z > 0)
+    def _():
+        greet(below)
+
+    pl.semaphore_wait(
+        barrier, 2 + jnp.where(z < depth - 1, 1, 0) + jnp.where(z > 0, 1, 0)
+    )
+
+    mine = pltpu.make_async_copy(own_ref, all_ref.at[rows(me)], own_sem)
+    mine.start()
+
+    @pl.when(z < depth - 1)
+    def _():
+        copy(me, 0, above, own_ref).start()
+
+    @pl.when(z > 0)
+    def _():
+        copy(me, 1, below, own_ref).start()
+
+    copy(me, 2, across, own_ref).start()
+    copy(me, 3, twin, own_ref).start()
+
+    for hop in range(1, depth):
+        low, high = me - 4 * hop, me + 4 * hop
+
+        @pl.when(z >= hop)
+        def _():
+            arrived(low)
+
+            @pl.when(z < depth - 1)
+            def _():
+                copy(low, 0, above).start()
+
+            copy(low, 2, across).start()
+            copy(low, 3, twin).start()
+
+        @pl.when(z + hop < depth)
+        def _():
+            arrived(high)
+
+            @pl.when(z > 0)
+            def _():
+                copy(high, 1, below).start()
+
+            copy(high, 2, across).start()
+            copy(high, 3, twin).start()
+
+        if hop == 1:
+            arrived(across)
+            copy(across, 3, twin).start()
+        else:
+            pass_on(across, hop - 1, z, depth, arrived, copy, twin)
+    pass_on(across, depth - 1, z, depth, arrived, copy, twin)
+
+    other = 1 - core
+    for block in range(depth * 2):
+        arrived(block * 2 + other)
+    mine.wait()
+    for up in range(depth):
+        block = up * 4 + y * 2 + core
+
+        @pl.when((up <= z) & (z < depth - 1))
+        def _():
+            copy(block, 0, above).wait_send()
+
+        @pl.when((up >= z) & (z > 0))
+        def _():
+            copy(block, 1, below).wait_send()
+
+        copy(block, 2, across).wait_send()
+        copy(block, 3, twin).wait_send()
+        copy(up * 4 + (1 - y) * 2 + core, 3, twin).wait_send()
+
+
+def pass_on(across, hop, z, depth, arrived, copy, twin):
+    @pl.when(z >= hop)
+    def _():
+        arrived(across - 4 * hop)
+        copy(across - 4 * hop, 3, twin).start()
+
+    @pl.when(z + hop < depth)
+    def _():
+        arrived(across + 4 * hop)
+        copy(across + 4 * hop, 3, twin).start()
+
+
+def run_gather(own, count):
+    return pl.pallas_call(
+        functools.partial(gather_kernel, count),
+        out_shape=jax.ShapeDtypeStruct((count * own.shape[0], own.shape[1]), own.dtype),
+        in_specs=[pl.BlockSpec(memory_space=pl.ANY)],
+        out_specs=pl.BlockSpec(memory_space=pl.ANY),
+        scratch_shapes=[
+            pltpu.SemaphoreType.DMA,
+            pltpu.SemaphoreType.DMA((count, 4)),
+            pltpu.SemaphoreType.DMA((count,)),
+        ],
+        compiler_params=pltpu.CompilerParams(collective_id=0, has_side_effects=True),
+        cost_estimate=pl.CostEstimate(
+            flops=0, bytes_accessed=8 * count * own.size, transcendentals=0
         ),
-    )(me, maps)
+    )(own)
 
 
 def finish_kernel(out_ref, lift_ref, state_ref, gain_ref, done_ref):
     for h in range(state_ref.shape[0]):
         cols = slice(h * DK, (h + 1) * DK)
-        o = out_ref[:, cols] + dot(lift_ref[:, cols], state_ref[h])
+        o = out_ref[:, cols] + dot_nt(lift_ref[:, cols], state_ref[h])
         mean = jnp.mean(o * o, axis=-1, keepdims=True)
         done_ref[:, cols] = (o * lax.rsqrt(mean + 1e-06) * gain_ref[...]).astype(BF)
 
@@ -250,6 +381,7 @@
 
 
 def shards(
+    n_seq,
     n_grp,
     prompt_tokens,
     response_tokens,
@@ -276,19 +408,21 @@
     columns = jnp.concatenate(
         [w_query, w_key, w_value, w_decay, w_beta, jnp.zeros((w_decay.shape[0], pad), BF)], axis=1
     )
-    weights = lax.all_gather(columns, "seq", axis=0, tiled=True)
+    weights = run_gather(columns, n_seq)
     length, depth = response_tokens.shape[2:]
     tokens = lax.all_gather(response_tokens.reshape(length, depth), "grp", axis=0, tiled=True)
 
     blocks = prompt_tokens.shape[0] // ROWS
     out, lifted, own_map = run_blocks(
-        prompt_tokens, weights, rate, shift, key_heads, value_heads, blocks
-    )
-    maps = lax.all_gather(own_map[None], "seq", axis=0, tiled=True)
+        prompt_tokens, weights, rate, shift, key_heads, value_heads, blocks, n_seq
+    )
+    maps = lax.all_to_all(own_map, "seq", split_axis=0, concat_axis=0, tiled=True)
     r_out, r_lifted, _ = run_blocks(
-        tokens, weights, rate, shift, key_heads, value_heads, length // ROWS
-    )
-    start, end = run_scan(lax.axis_index("seq").reshape(1), maps)
+        tokens, weights, rate, shift, key_heads, value_heads, length // ROWS, value_heads
+    )
+    states = lax.all_to_all(run_scan(maps), "seq", split_axis=0, concat_axis=0, tiled=True)
+    start = states[:, 0].reshape(value_heads, DK, DK)
+    end = states[:, 1].reshape(value_heads, DK, DK)
     r_done = run_finish(r_out, r_lifted, end, gain).reshape(n_grp, length, -1)
     prompt_output = run_finish(out, lifted, start, gain)
     exchanged = lax.all_to_all(r_done, "grp", split_axis=0, concat_axis=0, tiled=True)
@@ -313,7 +447,7 @@
         P("grp", "seq"),
     )
     return jax.shard_map(
-        functools.partial(shards, mesh.shape["grp"]),
+        functools.partial(shards, mesh.shape["seq"], mesh.shape["grp"]),
         mesh=mesh,
         in_specs=placed,
         out_specs=(P("seq", "grp"), P("grp", "seq", None, None)),

time: 246 us -> 203 us (0.83)
  waiting for transfers between devices: 133 us -> 8.85 us
  Pallas kernels: 75.6 us -> 128 us
  blocking collectives: 0 us -> 26 us
  starting transfers between devices: 3.7 us -> 8.37 us
    all_gather x2 -> x0, waiting for transfers between devices: 124 us -> none  [the longest x1 76.4 us: shards(): weights = lax.all_gather(columns, 'seq', axis=0, tiled=True)]
    pallas_call x1 -> x2, Pallas kernels: 5.08 us -> 57.8 us  [the longest x1 54.8 us: run_gather(): pl.pallas_call(functools.partial(gather_kernel, count), out_shape=jax.Sha...]
    all_to_all x0 -> x1, blocking collectives: none -> 26 us  [shards(): lax.all_to_all(own_map, 'seq', split_axis=0, concat_axis=0, tiled=True)]
    all_to_all x0 -> x1, starting transfers between devices: none -> 4.75 us  [shards(): lax.all_to_all(run_scan(maps), 'seq', split_axis=0, concat_axis=0, tiled=...]
    unnamed x14 -> x16, local copies, waits for them, and re-layouts: 10.1 us -> 8.28 us
  transfers between devices with their start and end apart: 4 -> 3, of which waited for: 3 -> 1; matrix products, arithmetic and copies ran while one was open for 1% -> 2% of each run, Pallas kernels for 28% -> 63%
where the time goes in v2:
time: 203 us; the launch traced here: 201 us
  Pallas kernels  128 us (63%)
  blocking collectives  26 us (13%)
  between operations  14.8 us (7%)
  local copies, waits for them, and re-layouts  13.4 us (7%)
  waiting for transfers between devices  8.85 us (4%)
  starting transfers between devices  8.37 us (4%)
    pallas_call x2, Pallas kernels, run_blocks(): pl.pallas_call(functools.partial(block_kernel, key_heads, value_heads, sp...  65.5 us
    pallas_call x1, Pallas kernels, run_gather(): pl.pallas_call(functools.partial(gather_kernel, count), out_shape=jax.Sha...  54.8 us
    all_to_all x1, blocking collectives, shards(): lax.all_to_all(own_map, 'seq', split_axis=0, concat_axis=0, tiled=True)  26 us
    unnamed x16, local copies, waits for them, and re-layouts  8.28 us
    all_to_all x1, waiting for transfers between devices, shards(): lax.all_to_all(r_done, 'grp', split_axis=0, concat_axis=0, tiled=True)  8.15 us
    pallas_call x2, Pallas kernels, run_finish(): pl.pallas_call(finish_kernel, grid=(count // ROWS,), in_specs=[rows, rows...  5.05 us
    all_to_all x1, starting transfers between devices, shards(): lax.all_to_all(run_scan(maps), 'seq', split_axis=0, concat_axis=0, tiled=...  4.75 us
  transfers between devices with their start and end apart: 3, of which 1 were waited for; matrix products, arithmetic and copies ran while one was open for 2% of the time, Pallas kernels for 63%

profile of v2, /device:TPU:8, one launch (start us, length us, event | category | flops | bytes accessed | tf_op | source)
XLA Modules:
  0.0 200.9 jit_solution(6966248131901116070)
XLA Ops:
  7.2 0.0 all-gather.3.cloned.1.call-start
  7.2 0.7 all-gather.3.cloned.1.call-update
  7.9 0.8 copy.13
  8.7 0.8 copy.14
  9.5 1.9 concatenate.3.own_ref
  11.4 0.0 copy-start.5
  11.4 0.0 copy-start.6
  11.4 54.8 %shard_map.122.w_ref = bf16[2048,2176]{1,0:T(8,128)(2,1)} custom-call(bf16[128,2176]{1,0:T(8,128)(2,1)} %concatenate.3.own_ref), custom_call_target="tpu_custom_call" | custom-call | bytes 35651584 | tf_op jit(solution)/shard_map/pallas_call | solution.py:335
  66.3 0.0 copy-done.5
  66.3 0.1 dynamic_slice.7
  66.4 0.0 copy-done.6
  66.4 0.1 dynamic_slice.6
  66.4 0.1 pad_bitcast_fusion
  66.5 42.4 %shard_map.123 = (f32[1024,1024]{1,0:T(8,128)}, bf16[1024,1024]{1,0:T(8,128)(2,1)S(1)}, bf16[16,192,128]{2,1,0:T(8,128)(2,1)S(1)}) custom-call(bf16[1024,2048]{1,0:T(8,128)(2,1)} %x_ref.1, bf16[2048,2176]{1,0:T(8,128)(2,1)} %shard_map.122.w_ref, f32[1,128]{1,0:T(1,128)S(1)} %get-tuple-element.15.rate_ref, f32[1,128]{1,0:T(1,128)S(1)} %get-tuple-element.14.shift_ref), custom_call_target="tpu_custom_call" | custom-call | flops 14579400704 | bytes 19398656 | tf_op jit(solution)/shard_map/pallas_call | solution.py:149
  108.9 26.0 %all_to_all.15.maps_ref = bf16[16,192,128]{2,1,0:T(8,128)(2,1)S(1)} all-to-all(bf16[16,192,128]{2,1,0:T(8,128)(2,1)S(1)} %get-tuple-element.9), channel_id=1, replica_groups=mesh['seq'=16,'grp'=2] {'seq'}, dimensions={0} | all-to-all | bytes 1572864 | tf_op jit(solution)/shard_map/all_to_all | solution.py:419
  135.0 2.9 %shard_map.124 = bf16[16,2,64,128]{3,2,1,0:T(8,128)(2,1)} custom-call(bf16[16,192,128]{2,1,0:T(8,128)(2,1)S(1)} %all_to_all.15.maps_ref), custom_call_target="tpu_custom_call" | custom-call | tf_op jit(solution)/shard_map/pallas_call | solution.py:198
  137.9 4.7 %all-to-all-start.1 = ((bf16[16,2,64,128]{3,2,1,0:T(8,128)(2,1)}), bf16[16,2,64,128]{3,2,1,0:T(8,128)(2,1)}, u32[]{:S(2)}, u32[]{:S(2)}) async-start(bf16[16,2,64,128]{3,2,1,0:T(8,128)(2,1)} %shard_map.124), calls=%async_computation.1 | async-start | bytes 1048576 | tf_op jit(solution)/shard_map/all_to_all | solution.py:423
  142.6 0.0 all-gather.3.cloned.1.call-done
  142.7 0.0 copy-start.4
  142.7 1.6 copy-done.4
  144.2 0.0 copy-start.3
  144.2 23.1 %shard_map.126 = (f32[512,1024]{1,0:T(8,128)S(1)}, bf16[512,1024]{1,0:T(8,128)(2,1)S(1)}, bf16[8,256,128]{2,1,0:T(8,128)(2,1)}) custom-call(bf16[512,2048]{1,0:T(8,128)(2,1)S(1)} %bitcast.16, bf16[2048,2176]{1,0:T(8,128)(2,1)} %shard_map.122.w_ref, f32[1,128]{1,0:T(1,128)S(1)} %get-tuple-element.15.rate_ref, f32[1,128]{1,0:T(1,128)S(1)} %get-tuple-element.14.shift_ref), custom_call_target="tpu_custom_call" | custom-call | flops 7289700352 | bytes 14155776 | tf_op jit(solution)/shard_map/pallas_call | solution.py:149
  167.4 0.0 copy-start.1
  167.4 1.3 copy-done.1
  168.7 0.0 all-to-all-done.1
  168.7 1.1 fusion
  169.7 0.0 copy-done.3
  169.8 0.0 copy-start.2
  169.8 1.6 copy-done.2
  171.4 1.9 shard_map.127
  173.2 3.6 %all-to-all-start.2 = ((bf16[2,256,1024]{2,1,0:T(8,128)(2,1)}), bf16[2,256,1024]{2,1,0:T(8,128)(2,1)S(1)}, u32[]{:S(2)}, u32[]{:S(2)}) async-start(bf16[2,256,1024]{2,1,0:T(8,128)(2,1)} %bitcast.7), calls=%async_computation.2 | async-start | bytes 2097152 | tf_op jit(solution)/shard_map/all_to_all | solution.py:428
  177.5 0.0 copy-start
  177.5 2.2 %copy-done = f32[1024,1024]{1,0:T(8,128)S(1)} copy-done((f32[1024,1024]{1,0:T(8,128)S(1)}, f32[1024,1024]{1,0:T(8,128)}, u32[]{:S(2)}) %copy-start) | copy-done | bytes 4194328
  179.7 3.2 %shard_map.125 = bf16[1024,1024]{1,0:T(8,128)(2,1)} custom-call(f32[1024,1024]{1,0:T(8,128)S(1)} %copy-done, bf16[1024,1024]{1,0:T(8,128)(2,1)S(1)} %get-tuple-element.8.lift_ref, bf16[8,128,128]{2,1,0:T(8,128)(2,1)S(1)} %bitcast.12, f32[1,128]{1,0:T(1,128)S(1)} %bitcast.15), custom_call_target="tpu_custom_call" | custom-call | flops 268435456 | bytes 8388608 | tf_op jit(solution)/shard_map/pallas_call | solution.py:363
  182.8 8.2 %all-to-all-done.2 = bf16[2,256,1024]{2,1,0:T(8,128)(2,1)S(1)} async-done(((bf16[2,256,1024]{2,1,0:T(8,128)(2,1)}), bf16[2,256,1024]{2,1,0:T(8,128)(2,1)S(1)}, u32[]{:S(2)}, u32[]{:S(2)}) %all-to-all-start.2) | async-done | bytes 1048608 | tf_op jit(solution)/shard_map/all_to_all | solution.py:428
  191.0 1.1 copy.15
  192.1 0.8 reshape.66
  192.9 1.1 broadcast_select_fusion
  (2 shorter events, 0.0 us)
Async XLA Ops:
  7.2 135.5 %all-gather.3.cloned.1.call-start = ((), (), s32[]{:S(2)}) async-start(), calls=%async_computation.3 | async-start | bytes 3145728 | tf_op jit(solution)/shard_map/all_gather | solution.py:413
  11.4 54.9 %copy-start.5 = (f32[16]{0:T(128)S(1)}, f32[16]{0:T(128)}, u32[]{:S(2)}) copy-start(f32[16]{0:T(128)} %param.19) | copy-start | bytes 196
  11.4 54.9 %copy-start.6 = (f32[16]{0:T(128)S(1)}, f32[16]{0:T(128)}, u32[]{:S(2)}) copy-start(f32[16]{0:T(128)} %param.18) | copy-start | bytes 196
  137.9 30.8 %all-to-all-start.1 = ((bf16[16,2,64,128]{3,2,1,0:T(8,128)(2,1)}), bf16[16,2,64,128]{3,2,1,0:T(8,128)(2,1)}, u32[]{:S(2)}, u32[]{:S(2)}) async-start(bf16[16,2,64,128]{3,2,1,0:T(8,128)(2,1)} %shard_map.124), calls=%async_computation.1 | async-start | bytes 1048576 | tf_op jit(solution)/shard_map/all_to_all | solution.py:423
  142.7 1.6 copy-start.4
  144.2 25.5 %copy-start.3 = (f32[128]{0:T(128)S(1)}, f32[128]{0:T(128)}, u32[]{:S(2)}) copy-start(f32[128]{0:T(128)} %param.20) | copy-start | bytes 1540
  167.4 1.3 copy-start.1
  169.8 1.6 copy-start.2
  173.2 17.8 %all-to-all-start.2 = ((bf16[2,256,1024]{2,1,0:T(8,128)(2,1)}), bf16[2,256,1024]{2,1,0:T(8,128)(2,1)S(1)}, u32[]{:S(2)}, u32[]{:S(2)}) async-start(bf16[2,256,1024]{2,1,0:T(8,128)(2,1)} %bitcast.7), calls=%async_computation.2 | async-start | bytes 2097152 | tf_op jit(solution)/shard_map/all_to_all | solution.py:428
  177.5 2.2 %copy-start = (f32[1024,1024]{1,0:T(8,128)S(1)}, f32[1024,1024]{1,0:T(8,128)}, u32[]{:S(2)}) copy-start(f32[1024,1024]{1,0:T(8,128)} %get-tuple-element.7.out_ref) | copy-start | bytes 12582916
Sparse Core Ops, SparseCore 0:
  9.5 34.2 all-gather.2

commit v3 on v2

--- a/solution.py
+++ b/solution.py
@@ -24,7 +24,7 @@
 
 
 def block_kernel(
-    key_heads, value_heads, span, x_ref, w_ref, rate_ref, shift_ref,
+    key_heads, value_heads, first, local, span, x_ref, w_ref, gate_ref, rate_ref, shift_ref,
     out_ref, lift_ref, map_ref, raw, carry,
 ):
     repeat = value_heads // key_heads
@@ -45,13 +45,14 @@
     for at in range(0, total, 512):
         size = min(512, total - at)
         raw[:, at:at + size] = dot(x, w_ref[:, at:at + size])
+    raw[:, total:] = dot(x, gate_ref[...])
 
     @pl.loop(0, ROWS // CHUNK)
     def _(c):
         rows = pl.ds(pl.multiple_of(c * CHUNK, CHUNK), CHUNK)
         within = row >= col
         differ = row ^ col
-        gates = raw[rows, total - LANES:]
+        gates = raw[rows, total:]
         log_decay = -rate_ref[...] * jax.nn.softplus(gates)
         beta = jax.nn.sigmoid(gates + shift_ref[...])
         lower_ones = jnp.where(within, 1.0, 0.0).astype(F32)
@@ -86,12 +87,13 @@
         lowers, inverses, scores = [], [], []
         for h in heads:
             both = dots[h // repeat]
-            spread = cumul[:, h:h + 1] - cumul_t[h:h + 1, :]
+            g = first + h
+            spread = cumul[:, g:g + 1] - cumul_t[g:g + 1, :]
             decay = jnp.where(within, jnp.exp(spread), 0.0)
             scores.append((decay * both[:CHUNK]).astype(BF))
             lower = jnp.where(
                 differ > 0,
-                beta[:, value_heads + h:value_heads + h + 1] * decay * both[CHUNK:],
+                beta[:, local + g:local + g + 1] * decay * both[CHUNK:],
                 0.0,
             )
             inverses.append(ident - jnp.where(differ == 1, lower, 0.0))
@@ -103,24 +105,27 @@
 
         solved = []
         for h in heads:
-            b_row = beta_t[value_heads + h:value_heads + h + 1, :]
+            g = first + h
+            b_row = beta_t[local + g:local + g + 1, :]
             scaled = inverses[h] * b_row
             at = (2 * key_heads + h) * DK
             values = raw[rows, at:at + DK].astype(BF)
             fresh = dot(scaled.astype(BF), values)
-            weights = dot((scaled * factor_t[h:h + 1, :]).astype(BF), keys[h // repeat])
+            weights = dot((scaled * factor_t[g:g + 1, :]).astype(BF), keys[h // repeat])
             solved.append(jnp.concatenate([weights, fresh], axis=1).astype(BF))
         parts = []
         for h in heads:
-            tails = (keys_t[h // repeat] * tail_t[h:h + 1, :]).astype(BF)
+            g = first + h
+            tails = (keys_t[h // repeat] * tail_t[g:g + 1, :]).astype(BF)
             parts.append(dot(jnp.concatenate([scores[h], tails], axis=0), solved[h]))
         for h in heads:
+            g = first + h
             part = parts[h]
-            lifted = factor[:, h:h + 1] * queries[h // repeat] - part[:CHUNK, :DK]
+            lifted = factor[:, g:g + 1] * queries[h // repeat] - part[:CHUNK, :DK]
             state = carry[h]
             left = jnp.concatenate([lifted, -part[CHUNK:, :DK]], axis=0).astype(BF)
             moved = dot(left, state.astype(BF))
-            last = factor[CHUNK - 1:, h:h + 1]
+            last = factor[CHUNK - 1:, g:g + 1]
             span_cols = slice(h * DK, (h + 1) * DK)
             out_ref[rows, span_cols] = moved[:CHUNK, DK:] + part[:CHUNK, DK:]
             lift_ref[rows, span_cols] = moved[:CHUNK, :DK].astype(BF)
@@ -140,18 +145,23 @@
                 map_ref[h * parts + p, DK:] = ends[p * width:(p + 1) * width]
 
 
-def run_blocks(x, weights, rate, shift, key_heads, value_heads, span, takers):
+def run_blocks(x, weights, gates, rate, shift, sizes, span, takers):
+    key_heads, value_heads, first, local = sizes
     count, depth = x.shape
-    total = weights.shape[1]
+    total = (2 * key_heads + value_heads) * DK
+    gate_block = gates.shape[1] // LANES - 1
     width = value_heads * DK
     map_rows = DK + DK * value_heads // takers
     whole = lambda shape: pl.BlockSpec(shape, lambda i: (0,) * len(shape))
     return pl.pallas_call(
-        functools.partial(block_kernel, key_heads, value_heads, span),
+        functools.partial(block_kernel, key_heads, value_heads, first, local, span),
         grid=(count // ROWS,),
         in_specs=[
             pl.BlockSpec((ROWS, depth), lambda i: (i, 0)),
             pl.BlockSpec((depth, total), lambda i: (0, 0), pipeline_mode=pl.Buffered(1)),
+            pl.BlockSpec(
+                (depth, LANES), lambda i: (0, gate_block), pipeline_mode=pl.Buffered(1)
+            ),
             whole((1, LANES)),
             whole((1, LANES)),
         ],
@@ -166,7 +176,7 @@
             jax.ShapeDtypeStruct((takers, map_rows, DK), BF),
         ],
         scratch_shapes=[
-            pltpu.VMEM((ROWS, total), F32),
+            pltpu.VMEM((ROWS, total + LANES), F32),
             pltpu.VMEM((value_heads, DK, 2 * DK), F32),
         ],
         compiler_params=pltpu.CompilerParams(
@@ -177,31 +187,35 @@
             bytes_accessed=2 * count * depth + 2 * depth * total + 6 * count * width,
             transcendentals=count * value_heads * DK,
         ),
-    )(x, weights, rate, shift)
-
-
-def scan_kernel(maps_ref, states_ref):
-    count, rows = maps_ref.shape[:2]
-    held = jnp.zeros((rows - DK, DK), F32)
+    )(x, weights, gates, rate, shift)
+
+
+def scan_kernel(*refs):
+    maps, states_ref = refs[:-1], refs[-1]
+    count, rows = maps[0].shape[:2]
+    width = rows - DK
+    held = [jnp.zeros((width, DK), F32) for _ in maps]
     for i in range(count):
-        states_ref[i, 0] = held.astype(BF)
-        high = held.astype(BF).astype(F32)
-        both = jnp.concatenate([high, held - high], axis=0).astype(BF)
-        moved = dot_nt(both, maps_ref[i, :DK])
-        held = held + (moved[:rows - DK] + moved[rows - DK:]) + maps_ref[i, DK:].astype(F32)
+        for p, ref in enumerate(maps):
+            states_ref[i, 2 * p] = held[p].astype(BF)
+            high = held[p].astype(BF).astype(F32)
+            both = jnp.concatenate([high, held[p] - high], axis=0).astype(BF)
+            moved = dot_nt(both, ref[i, :DK])
+            held[p] = held[p] + (moved[:width] + moved[width:]) + ref[i, DK:].astype(F32)
     for i in range(count):
-        states_ref[i, 1] = held.astype(BF)
+        for p in range(len(maps)):
+            states_ref[i, 2 * p + 1] = held[p].astype(BF)
 
 
 def run_scan(maps):
-    count, rows = maps.shape[:2]
+    count, rows = maps[0].shape[:2]
     return pl.pallas_call(
         scan_kernel,
-        out_shape=jax.ShapeDtypeStruct((count, 2, rows - DK, DK), BF),
-        in_specs=[pl.BlockSpec(memory_space=pltpu.VMEM)],
+        out_shape=jax.ShapeDtypeStruct((count, 2 * len(maps), rows - DK, DK), BF),
+        in_specs=[pl.BlockSpec(memory_space=pltpu.VMEM)] * len(maps),
         out_specs=pl.BlockSpec(memory_space=pltpu.VMEM),
         compiler_params=pltpu.CompilerParams(vmem_limit_bytes=16 * 1024 * 1024),
-    )(maps)
+    )(*maps)
 
 
 def gather_kernel(count, own_ref, all_ref, own_sem, send_sems, recv_sems):
@@ -349,27 +363,31 @@
     )(own)
 
 
-def finish_kernel(out_ref, lift_ref, state_ref, gain_ref, done_ref):
-    for h in range(state_ref.shape[0]):
-        cols = slice(h * DK, (h + 1) * DK)
-        o = out_ref[:, cols] + dot_nt(lift_ref[:, cols], state_ref[h])
-        mean = jnp.mean(o * o, axis=-1, keepdims=True)
-        done_ref[:, cols] = (o * lax.rsqrt(mean + 1e-06) * gain_ref[...]).astype(BF)
-
-
-def run_finish(out, lifted, state, gain):
-    count, width = out.shape
-    rows = pl.BlockSpec((ROWS, width), lambda i: (i, 0))
+def finish_kernel(*refs):
+    gain_ref, done_ref = refs[-2:]
+    parts = (len(refs) - 2) // 3
+    outs, lifts, states = refs[:parts], refs[parts:2 * parts], refs[2 * parts:3 * parts]
+    at = 0
+    for out_ref, lift_ref, state_ref in zip(outs, lifts, states):
+        for h in range(state_ref.shape[0]):
+            cols = slice(h * DK, (h + 1) * DK)
+            o = out_ref[:, cols] + dot_nt(lift_ref[:, cols], state_ref[h])
+            mean = jnp.mean(o * o, axis=-1, keepdims=True)
+            done_ref[:, at:at + DK] = (o * lax.rsqrt(mean + 1e-06) * gain_ref[...]).astype(BF)
+            at += DK
+
+
+def run_finish(outs, lifts, states, gain):
+    count = outs[0].shape[0]
+    width = sum(o.shape[1] for o in outs)
+    rows = [pl.BlockSpec((ROWS, o.shape[1]), lambda i: (i, 0)) for o in outs]
     return pl.pallas_call(
         finish_kernel,
         grid=(count // ROWS,),
-        in_specs=[
-            rows,
-            rows,
-            pl.BlockSpec(state.shape, lambda i: (0, 0, 0)),
-            pl.BlockSpec((1, DK), lambda i: (0, 0)),
-        ],
-        out_specs=rows,
+        in_specs=rows + rows
+        + [pl.BlockSpec(s.shape, lambda i: (0, 0, 0)) for s in states]
+        + [pl.BlockSpec((1, DK), lambda i: (0, 0))],
+        out_specs=pl.BlockSpec((ROWS, width), lambda i: (i, 0)),
         out_shape=jax.ShapeDtypeStruct((count, width), BF),
         compiler_params=pltpu.CompilerParams(
             dimension_semantics=("arbitrary",), vmem_limit_bytes=32 * 1024 * 1024
@@ -377,7 +395,7 @@
         cost_estimate=pl.CostEstimate(
             flops=2 * count * width * DK, bytes_accessed=8 * count * width, transcendentals=0
         ),
-    )(out, lifted, state, gain)
+    )(*outs, *lifts, *states, gain)
 
 
 def shards(
@@ -405,26 +423,45 @@
     rate = jnp.pad(rate, (0, LANES - value_heads)).reshape(1, LANES)
     shift = jnp.pad(shift, (value_heads, pad)).reshape(1, LANES)
     gain = out_gain.reshape(1, DK)
-    columns = jnp.concatenate(
-        [w_query, w_key, w_value, w_decay, w_beta, jnp.zeros((w_decay.shape[0], pad), BF)], axis=1
-    )
-    weights = run_gather(columns, n_seq)
+    parts = 2 if key_heads % 2 == 0 else 1
+    part_heads = value_heads // parts
+
+    def part_of(array, part):
+        size = array.shape[1] // parts
+        return array[:, part * size:(part + 1) * size]
+
+    columns = [[part_of(w, p) for w in (w_query, w_key, w_value)] for p in range(parts)]
+    columns[0] += [w_decay, w_beta, jnp.zeros((w_decay.shape[0], pad), BF)]
+    columns = [jnp.concatenate(group, axis=1) for group in columns]
+    weights = [run_gather(columns[0], n_seq)]
+    weights += [lax.all_gather(c, "seq", axis=0, tiled=True) for c in columns[1:]]
     length, depth = response_tokens.shape[2:]
     tokens = lax.all_gather(response_tokens.reshape(length, depth), "grp", axis=0, tiled=True)
 
+    def blocks_of(x, part, span, takers):
+        sizes = (key_heads // parts, part_heads, part * part_heads, value_heads)
+        return run_blocks(x, weights[part], weights[0], rate, shift, sizes, span, takers)
+
     blocks = prompt_tokens.shape[0] // ROWS
-    out, lifted, own_map = run_blocks(
-        prompt_tokens, weights, rate, shift, key_heads, value_heads, blocks, n_seq
-    )
-    maps = lax.all_to_all(own_map, "seq", split_axis=0, concat_axis=0, tiled=True)
-    r_out, r_lifted, _ = run_blocks(
-        tokens, weights, rate, shift, key_heads, value_heads, length // ROWS, value_heads
-    )
-    states = lax.all_to_all(run_scan(maps), "seq", split_axis=0, concat_axis=0, tiled=True)
-    start = states[:, 0].reshape(value_heads, DK, DK)
-    end = states[:, 1].reshape(value_heads, DK, DK)
-    r_done = run_finish(r_out, r_lifted, end, gain).reshape(n_grp, length, -1)
-    prompt_output = run_finish(out, lifted, start, gain)
+    outs, lifts, maps, r_outs, r_lifts = [], [], [], [], []
+    for p in range(parts):
+        out, lifted, own_map = blocks_of(prompt_tokens, p, blocks, n_seq)
+        outs.append(out)
+        lifts.append(lifted)
+        maps.append(lax.all_to_all(own_map, "seq", split_axis=0, concat_axis=0, tiled=True))
+    for p in range(parts):
+        if p == parts - 1:
+            maps, r_outs, r_lifts = lax.optimization_barrier((maps, r_outs, r_lifts))
+            chained = run_scan(maps)
+            chained, tokens = lax.optimization_barrier((chained, tokens))
+            states = lax.all_to_all(chained, "seq", split_axis=0, concat_axis=0, tiled=True)
+        r_out, r_lifted, _ = blocks_of(tokens, p, length // ROWS, part_heads)
+        r_outs.append(r_out)
+        r_lifts.append(r_lifted)
+    starts = [states[:, 2 * p].reshape(part_heads, DK, DK) for p in range(parts)]
+    ends = [states[:, 2 * p + 1].reshape(part_heads, DK, DK) for p in range(parts)]
+    r_done = run_finish(r_outs, r_lifts, ends, gain).reshape(n_grp, length, -1)
+    prompt_output = run_finish(outs, lifts, starts, gain)
     exchanged = lax.all_to_all(r_done, "grp", split_axis=0, concat_axis=0, tiled=True)
     finished = jnp.swapaxes(exchanged, 0, 1).reshape(length, -1)
     positions = lax.broadcasted_iota(jnp.int32, (length, 1), 0)

time: 203 us -> 234 us (1.15)
  blocking collectives: 26 us -> 0 us
  starting transfers between devices: 8.37 us -> 33.1 us
  Pallas kernels: 128 us -> 146 us
  local copies, waits for them, and re-layouts: 13.4 us -> 28 us
    pallas_call x5 -> x7, Pallas kernels: 73.5 us -> 106 us  [the longest x4 98.5 us: run_blocks(): pl.pallas_call(functools.partial(block_kernel, key_heads, value_heads, fi...]
    all_to_all x1 -> x0, blocking collectives: 26 us -> none  [shards(): lax.all_to_all(own_map, 'seq', split_axis=0, concat_axis=0, tiled=True)]
    all_to_all x1 -> x3, starting transfers between devices: 4.75 us -> 28.5 us  [the longest x2 22.3 us: shards(): lax.all_to_all(own_map, 'seq', split_axis=0, concat_axis=0, tiled=True)]
    pallas_call x1, Pallas kernels: 54.8 us -> 40.4 us  [run_gather(): pl.pallas_call(functools.partial(gather_kernel, count), out_shape=jax.Sha...]
    unnamed x16 -> x40, local copies, waits for them, and re-layouts: 8.28 us -> 19.4 us
  transfers between devices with their start and end apart: 3 -> 6, of which waited for: 1 -> 1; matrix products, arithmetic and copies ran while one was open for 2% -> 2% of each run, Pallas kernels for 63% -> 61%
where the time goes in v3:
time: 234 us; the launch traced here: 232 us
  Pallas kernels  146 us (62%)
  starting transfers between devices  33.1 us (14%)
  local copies, waits for them, and re-layouts  28 us (12%)
  between operations  14.9 us (6%)
  waiting for transfers between devices  8.37 us (4%)
    pallas_call x4, Pallas kernels, run_blocks(): pl.pallas_call(functools.partial(block_kernel, key_heads, value_heads, fi...  98.5 us
    pallas_call x1, Pallas kernels, run_gather(): pl.pallas_call(functools.partial(gather_kernel, count), out_shape=jax.Sha...  40.4 us
    all_to_all x2, starting transfers between devices, shards(): lax.all_to_all(own_map, 'seq', split_axis=0, concat_axis=0, tiled=True)  22.3 us
    unnamed x40, local copies, waits for them, and re-layouts  19.4 us
    all_to_all x1, waiting for transfers between devices, shards(): lax.all_to_all(r_done, 'grp', split_axis=0, concat_axis=0, tiled=True)  7.62 us
    all_to_all x1, starting transfers between devices, shards(): lax.all_to_all(chained, 'seq', split_axis=0, concat_axis=0, tiled=True)  6.19 us
    pallas_call x2, Pallas kernels, run_finish(): pl.pallas_call(finish_kernel, grid=(count // ROWS,), in_specs=rows + rows...  5.01 us
  transfers between devices with their start and end apart: 6, of which 1 were waited for; matrix products, arithmetic and copies ran while one was open for 2% of the time, Pallas kernels for 61%

profile of v3, /device:TPU:8, one launch (start us, length us, event | category | flops | bytes accessed | tf_op | source)
XLA Modules:
  0.0 232.1 jit_solution(15161053704921999609)
XLA Ops:
  7.2 0.0 all-gather.4.cloned.1.call-start
  7.2 1.0 fusion.1
  8.2 1.0 fusion.2
  9.2 0.7 pad_maximum_fusion
  9.9 0.0 all-gather.4.cloned.1.call-update
  9.9 0.7 dynamic_slice.6
  10.7 0.7 dynamic_slice.7
  11.4 0.8 copy.13
  12.2 0.8 copy.14
  13.0 0.8 concatenate.6.own_ref
  13.8 40.4 %shard_map.122.w_ref.gate_ref = bf16[2048,1152]{1,0:T(8,128)(2,1)} custom-call(bf16[128,1152]{1,0:T(8,128)(2,1)} %concatenate.6.own_ref), custom_call_target="tpu_custom_call" | custom-call | bytes 18874368 | tf_op jit(solution)/shard_map/pallas_call | solution.py:349
  54.2 0.1 pad_bitcast_fusion
  54.3 32.3 %shard_map.123 = (f32[1024,512]{1,0:T(8,128)S(1)}, bf16[1024,512]{1,0:T(8,128)(2,1)S(1)}, bf16[16,160,128]{2,1,0:T(8,128)(2,1)}) custom-call(bf16[1024,2048]{1,0:T(8,128)(2,1)} %x_ref.3, bf16[2048,1152]{1,0:T(8,128)(2,1)} %shard_map.122.w_ref.gate_ref, bf16[2048,1152]{1,0:T(8,128)(2,1)} %shard_map.122.w_ref.gate_ref, ...), custom_call_target="tpu_custom_call" | custom-call | flops 7021264896 | bytes 11534336 | tf_op jit(solution)/shard_map/pallas_call | solution.py:156
  86.5 0.0 copy-start.3
  86.5 1.0 copy-done.3
  87.5 16.3 %all-to-all-start = ((bf16[16,160,128]{2,1,0:T(8,128)(2,1)}), bf16[16,160,128]{2,1,0:T(8,128)(2,1)S(1)}, u32[]{:S(2)}, u32[]{:S(2)}) async-start(bf16[16,160,128]{2,1,0:T(8,128)(2,1)} %get-tuple-element.22), calls=%async_computation | async-start | bytes 1310720 | tf_op jit(solution)/shard_map/all_to_all | solution.py:451
  103.8 0.0 all-gather.6.cloned.1.call-start
  103.8 0.7 all-gather.6.cloned.1.call-update
  104.5 0.0 all-gather.4.cloned.1.call-done.w_ref
  104.6 31.4 %shard_map.124 = (f32[1024,512]{1,0:T(8,128)S(1)}, bf16[1024,512]{1,0:T(8,128)(2,1)S(1)}, bf16[16,160,128]{2,1,0:T(8,128)(2,1)S(1)}) custom-call(bf16[1024,2048]{1,0:T(8,128)(2,1)} %x_ref.3, bf16[2048,1024]{1,0:T(8,128)(2,1)} %all-gather.4.cloned.1.call-done.w_ref, bf16[2048,1152]{1,0:T(8,128)(2,1)} %shard_map.122.w_ref.gate_ref, ...), custom_call_target="tpu_custom_call" | custom-call | flops 7021264896 | bytes 11534336 | tf_op jit(solution)/shard_map/pallas_call | solution.py:156
  135.9 0.0 copy-start
  135.9 1.3 copy-done
  137.3 0.0 copy-start.5
  137.3 1.0 copy-done.5
  138.2 0.0 copy-start.11
  138.2 0.8 copy-done.11
  139.1 0.0 all-to-all-done.refs_0_
  139.1 6.0 %all-to-all-start.1 = ((bf16[16,160,128]{2,1,0:T(8,128)(2,1)}), bf16[16,160,128]{2,1,0:T(8,128)(2,1)S(1)}, u32[]{:S(2)}, u32[]{:S(2)}) async-start(bf16[16,160,128]{2,1,0:T(8,128)(2,1)} %copy-done.11), calls=%async_computation.1 | async-start | bytes 1310720 | tf_op jit(solution)/shard_map/all_to_all | solution.py:451
  145.1 0.0 all-gather.6.cloned.1.call-done
  145.1 0.0 copy-start.17
  145.1 1.6 copy-done.17
  146.7 17.4 %shard_map.125 = (f32[512,512]{1,0:T(8,128)S(1)}, bf16[512,512]{1,0:T(8,128)(2,1)S(1)}, bf16[4,256,128]{2,1,0:T(8,128)(2,1)}) custom-call(bf16[512,2048]{1,0:T(8,128)(2,1)S(1)} %bitcast.20, bf16[2048,1152]{1,0:T(8,128)(2,1)} %shard_map.122.w_ref.gate_ref, bf16[2048,1152]{1,0:T(8,128)(2,1)} %shard_map.122.w_ref.gate_ref, ...), custom_call_target="tpu_custom_call" | custom-call | flops 3510632448 | bytes 7864320 | tf_op jit(solution)/shard_map/pallas_call | solution.py:156
  164.1 0.0 copy-start.7
  164.1 1.0 copy-done.7
  165.1 0.0 copy-start.12
  165.1 0.8 copy-done.12
  165.9 0.0 all-to-all-done.1.refs_1_
  165.9 2.0 shard_map.126
  168.0 0.0 copy-start.2
  168.0 0.8 copy-done.2
  168.8 6.2 %all-to-all-start.2 = ((bf16[16,4,32,128]{3,2,1,0:T(8,128)(2,1)}), bf16[16,4,32,128]{3,2,1,0:T(8,128)(2,1)}, u32[]{:S(2)}, u32[]{:S(2)}) async-start(bf16[16,4,32,128]{3,2,1,0:T(8,128)(2,1)} %copy-done.2), calls=%async_computation.2 | async-start | bytes 1048576 | tf_op jit(solution)/shard_map/all_to_all | solution.py:457
  175.0 1.6 copy-done.18
  176.6 17.5 %shard_map.128 = (f32[512,512]{1,0:T(8,128)S(1)}, bf16[512,512]{1,0:T(8,128)(2,1)S(1)}, bf16[4,256,128]{2,1,0:T(8,128)(2,1)}) custom-call(bf16[512,2048]{1,0:T(8,128)(2,1)S(1)} %bitcast.21, bf16[2048,1024]{1,0:T(8,128)(2,1)} %all-gather.4.cloned.1.call-done.w_ref, bf16[2048,1152]{1,0:T(8,128)(2,1)} %shard_map.122.w_ref.gate_ref, ...), custom_call_target="tpu_custom_call" | custom-call | flops 3510632448 | bytes 7864320 | tf_op jit(solution)/shard_map/pallas_call | solution.py:156
  194.0 1.0 copy-done.9
  195.1 0.8 copy-done.14
  195.9 0.0 all-to-all-done.2
  195.9 1.1 fusion
  197.0 0.0 copy-done.8
  197.0 0.0 copy-done.16
  197.0 0.0 copy-start.10
  197.0 1.2 copy-done.10
  198.3 1.0 copy-done.13
  199.3 1.0 copy-done.15
  200.3 1.9 shard_map.129
  202.2 4.5 %all-to-all-start.3 = ((bf16[2,256,1024]{2,1,0:T(8,128)(2,1)}), bf16[2,256,1024]{2,1,0:T(8,128)(2,1)}, u32[]{:S(2)}, u32[]{:S(2)}) async-start(bf16[2,256,1024]{2,1,0:T(8,128)(2,1)} %bitcast.9), calls=%async_computation.3 | async-start | bytes 2097152 | tf_op jit(solution)/shard_map/all_to_all | solution.py:465
  207.4 0.0 copy-done.4
  207.4 0.0 copy-start.1
  207.4 1.6 copy-done.1
  209.0 1.2 copy-done.6
  210.2 3.2 %shard_map.127 = bf16[1024,1024]{1,0:T(8,128)(2,1)} custom-call(f32[1024,512]{1,0:T(8,128)S(1)} %get-tuple-element.18.refs_0_, f32[1024,512]{1,0:T(8,128)S(1)} %copy-done.1, bf16[1024,512]{1,0:T(8,128)(2,1)S(1)} %copy-done.4, bf16[1024,512]{1,0:T(8,128)(2,1)S(1)} %copy-done.6, bf16[4,128,128]{2,1,0:T(8,128)(2,1)S(1)} %bitcast.15, ...), custom_call_target="tpu_custom_call" | custom-call | flops 268435456 | bytes 8388608 | tf_op jit(solution)/shard_map/pallas_call | solution.py:384
  213.4 7.6 %all-to-all-done.3 = bf16[2,256,1024]{2,1,0:T(8,128)(2,1)} async-done(((bf16[2,256,1024]{2,1,0:T(8,128)(2,1)}), bf16[2,256,1024]{2,1,0:T(8,128)(2,1)}, u32[]{:S(2)}, u32[]{:S(2)}) %all-to-all-start.3) | async-done | bytes 1048608 | tf_op jit(solution)/shard_map/all_to_all | solution.py:465
  221.0 2.3 copy.15
  223.3 0.8 reshape.66
  224.2 1.1 broadcast_select_fusion
  (11 shorter events, 0.0 us)
Async XLA Ops:
  7.2 97.4 %all-gather.4.cloned.1.call-start = ((), (), s32[]{:S(2)}) async-start(), calls=%async_computation.4 | async-start | bytes 4456448 | tf_op jit(solution)/shard_map/all_gather | solution.py:437
  86.5 1.0 copy-start.3
  87.5 51.6 %all-to-all-start = ((bf16[16,160,128]{2,1,0:T(8,128)(2,1)}), bf16[16,160,128]{2,1,0:T(8,128)(2,1)S(1)}, u32[]{:S(2)}, u32[]{:S(2)}) async-start(bf16[16,160,128]{2,1,0:T(8,128)(2,1)} %get-tuple-element.22), calls=%async_computation | async-start | bytes 1310720 | tf_op jit(solution)/shard_map/all_to_all | solution.py:451
  103.8 41.3 %all-gather.6.cloned.1.call-start = ((), (), s32[]{:S(2)}) async-start(), calls=%async_computation.5 | async-start | bytes 3145728 | tf_op jit(solution)/shard_map/all_gather | solution.py:439
  135.9 1.3 copy-start
  137.3 1.0 copy-start.5
  138.2 0.8 copy-start.11
  139.1 26.8 %all-to-all-start.1 = ((bf16[16,160,128]{2,1,0:T(8,128)(2,1)}), bf16[16,160,128]{2,1,0:T(8,128)(2,1)S(1)}, u32[]{:S(2)}, u32[]{:S(2)}) async-start(bf16[16,160,128]{2,1,0:T(8,128)(2,1)} %copy-done.11), calls=%async_computation.1 | async-start | bytes 1310720 | tf_op jit(solution)/shard_map/all_to_all | solution.py:451
  145.1 1.6 copy-start.17
  164.1 1.0 copy-start.7
  165.1 0.8 copy-start.12
  168.0 0.8 copy-start.2
  168.8 27.1 %all-to-all-start.2 = ((bf16[16,4,32,128]{3,2,1,0:T(8,128)(2,1)}), bf16[16,4,32,128]{3,2,1,0:T(8,128)(2,1)}, u32[]{:S(2)}, u32[]{:S(2)}) async-start(bf16[16,4,32,128]{3,2,1,0:T(8,128)(2,1)} %copy-done.2), calls=%async_computation.2 | async-start | bytes 1048576 | tf_op jit(solution)/shard_map/all_to_all | solution.py:457
  175.0 1.6 copy-start.18
  176.6 20.4 %copy-start.8 = (f32[512,512]{1,0:T(8,128)S(1)}, f32[512,512]{1,0:T(8,128)}, u32[]{:S(2)}) copy-start(f32[512,512]{1,0:T(8,128)} %copy-done.7) | copy-start | bytes 3145732
  176.6 20.4 %copy-start.16 = (f32[128]{0:T(128)S(1)}, f32[128]{0:T(128)}, u32[]{:S(2)}) copy-start(f32[128]{0:T(128)} %param.20) | copy-start | bytes 1540
  194.0 1.0 copy-start.9
  195.1 0.8 copy-start.14
  197.0 1.2 copy-start.10
  198.3 1.0 copy-start.13
  199.3 1.0 copy-start.15
  202.2 5.2 %copy-start.4 = (bf16[1024,512]{1,0:T(8,128)(2,1)S(1)}, bf16[1024,512]{1,0:T(8,128)(2,1)}, u32[]{:S(2)}) copy-start(bf16[1024,512]{1,0:T(8,128)(2,1)} %copy-done.3) | copy-start | bytes 3145732
  202.2 18.8 %all-to-all-start.3 = ((bf16[2,256,1024]{2,1,0:T(8,128)(2,1)}), bf16[2,256,1024]{2,1,0:T(8,128)(2,1)}, u32[]{:S(2)}, u32[]{:S(2)}) async-start(bf16[2,256,1024]{2,1,0:T(8,128)(2,1)} %bitcast.9), calls=%async_computation.3 | async-start | bytes 2097152 | tf_op jit(solution)/shard_map/all_to_all | solution.py:465
  207.4 1.6 copy-start.1
  209.0 1.2 copy-start.6
Sparse Core Ops, SparseCore 0:
  10.7 60.8 all-gather.3
  106.2 34.1 all-gather.5

commit v4 on v2

--- a/solution.py
+++ b/solution.py
@@ -46,98 +46,108 @@
         size = min(512, total - at)
         raw[:, at:at + size] = dot(x, w_ref[:, at:at + size])
 
-    @pl.loop(0, ROWS // CHUNK)
-    def _(c):
-        rows = pl.ds(pl.multiple_of(c * CHUNK, CHUNK), CHUNK)
-        within = row >= col
-        differ = row ^ col
+    within = row >= col
+    differ = row ^ col
+    lower_ones = jnp.where(within, 1.0, 0.0).astype(F32)
+    masks = []
+    size = 2
+    while size < CHUNK:
+        masks.append(
+            jnp.where((differ >= size) & (differ < 2 * size) & within, 1.0, 0.0).astype(BF)
+        )
+        size *= 2
+
+    chunks = range(ROWS // CHUNK)
+    both_of = [(c, h) for c in chunks for h in heads]
+    gates_of, queries, keys, keys_t, dots = [], {}, {}, {}, {}
+    for c in chunks:
+        rows = slice(c * CHUNK, (c + 1) * CHUNK)
         gates = raw[rows, total - LANES:]
         log_decay = -rate_ref[...] * jax.nn.softplus(gates)
         beta = jax.nn.sigmoid(gates + shift_ref[...])
-        lower_ones = jnp.where(within, 1.0, 0.0).astype(F32)
         cumul = jnp.dot(
             lower_ones, log_decay, preferred_element_type=F32, precision=lax.Precision.HIGHEST
         )
         cumul_t = cumul.T
-        beta_t = beta.T
-        factor = jnp.exp(cumul)
-        factor_t = jnp.exp(cumul_t)
-        tail_t = jnp.exp(cumul_t[:, CHUNK - 1:] - cumul_t)
-        masks = []
-        size = 2
-        while size < CHUNK:
-            masks.append(
-                jnp.where((differ >= size) & (differ < 2 * size) & within, 1.0, 0.0).astype(BF)
+        gates_of.append(
+            (
+                beta,
+                beta.T,
+                cumul,
+                cumul_t,
+                jnp.exp(cumul),
+                jnp.exp(cumul_t),
+                jnp.exp(cumul_t[:, CHUNK - 1:] - cumul_t),
             )
-            size *= 2
-
-        queries, keys, keys_t, dots = [], [], [], []
+        )
         for j in range(key_heads):
             q = raw[rows, j * DK:(j + 1) * DK]
             k = raw[rows, (key_heads + j) * DK:(key_heads + j + 1) * DK]
             q = q * lax.rsqrt(jnp.sum(q * q, axis=-1, keepdims=True) + 1e-06) * DK ** (-0.5)
             k = k * lax.rsqrt(jnp.sum(k * k, axis=-1, keepdims=True) + 1e-06)
             q, k = q.astype(BF), k.astype(BF)
-            queries.append(q.astype(F32))
-            keys.append(k)
-            keys_t.append(k.astype(F32).T)
-            dots.append(dot_nt(jnp.concatenate([q, k], axis=0), k))
-
-        lowers, inverses, scores = [], [], []
-        for h in heads:
-            both = dots[h // repeat]
-            spread = cumul[:, h:h + 1] - cumul_t[h:h + 1, :]
-            decay = jnp.where(within, jnp.exp(spread), 0.0)
-            scores.append((decay * both[:CHUNK]).astype(BF))
-            lower = jnp.where(
-                differ > 0,
-                beta[:, value_heads + h:value_heads + h + 1] * decay * both[CHUNK:],
-                0.0,
-            )
-            inverses.append(ident - jnp.where(differ == 1, lower, 0.0))
-            lowers.append(lower.astype(BF))
-        for mask in masks:
-            small = [x.astype(BF) for x in inverses]
-            mids = [dot(lowers[h] * mask, small[h]).astype(BF) for h in heads]
-            inverses = [inverses[h] - dot(small[h], mids[h]) for h in heads]
-
-        solved = []
-        for h in heads:
-            b_row = beta_t[value_heads + h:value_heads + h + 1, :]
-            scaled = inverses[h] * b_row
-            at = (2 * key_heads + h) * DK
-            values = raw[rows, at:at + DK].astype(BF)
-            fresh = dot(scaled.astype(BF), values)
-            weights = dot((scaled * factor_t[h:h + 1, :]).astype(BF), keys[h // repeat])
-            solved.append(jnp.concatenate([weights, fresh], axis=1).astype(BF))
-        parts = []
-        for h in heads:
-            tails = (keys_t[h // repeat] * tail_t[h:h + 1, :]).astype(BF)
-            parts.append(dot(jnp.concatenate([scores[h], tails], axis=0), solved[h]))
-        for h in heads:
-            part = parts[h]
-            lifted = factor[:, h:h + 1] * queries[h // repeat] - part[:CHUNK, :DK]
-            state = carry[h]
-            left = jnp.concatenate([lifted, -part[CHUNK:, :DK]], axis=0).astype(BF)
-            moved = dot(left, state.astype(BF))
-            last = factor[CHUNK - 1:, h:h + 1]
-            span_cols = slice(h * DK, (h + 1) * DK)
-            out_ref[rows, span_cols] = moved[:CHUNK, DK:] + part[:CHUNK, DK:]
-            lift_ref[rows, span_cols] = moved[:CHUNK, :DK].astype(BF)
-            fresh_state = last * state + moved[CHUNK:]
-            carry[h, :, :DK] = fresh_state[:, :DK]
-            carry[h, :, DK:] = fresh_state[:, DK:] + part[CHUNK:, DK:]
+            queries[c, j] = q.astype(F32)
+            keys[c, j] = k
+            keys_t[c, j] = k.astype(F32).T
+            dots[c, j] = dot_nt(jnp.concatenate([q, k], axis=0), k)
+
+    lowers, inverses, scores = {}, {}, {}
+    for c, h in both_of:
+        beta, _, cumul, cumul_t = gates_of[c][:4]
+        both = dots[c, h // repeat]
+        spread = cumul[:, h:h + 1] - cumul_t[h:h + 1, :]
+        decay = jnp.where(within, jnp.exp(spread), 0.0)
+        scores[c, h] = (decay * both[:CHUNK]).astype(BF)
+        lower = jnp.where(
+            differ > 0,
+            beta[:, value_heads + h:value_heads + h + 1] * decay * both[CHUNK:],
+            0.0,
+        )
+        inverses[c, h] = ident - jnp.where(differ == 1, lower, 0.0)
+        lowers[c, h] = lower.astype(BF)
+    for mask in masks:
+        small = {i: inverses[i].astype(BF) for i in both_of}
+        mids = {i: dot(lowers[i] * mask, small[i]).astype(BF) for i in both_of}
+        inverses = {i: inverses[i] - dot(small[i], mids[i]) for i in both_of}
+
+    solved, parts = {}, {}
+    for c, h in both_of:
+        beta_t, factor_t = gates_of[c][1], gates_of[c][5]
+        scaled = inverses[c, h] * beta_t[value_heads + h:value_heads + h + 1, :]
+        at = (2 * key_heads + h) * DK
+        values = raw[c * CHUNK:(c + 1) * CHUNK, at:at + DK].astype(BF)
+        fresh = dot(scaled.astype(BF), values)
+        weights = dot((scaled * factor_t[h:h + 1, :]).astype(BF), keys[c, h // repeat])
+        solved[c, h] = jnp.concatenate([weights, fresh], axis=1).astype(BF)
+    for c, h in both_of:
+        tail_t = gates_of[c][6]
+        tails = (keys_t[c, h // repeat] * tail_t[h:h + 1, :]).astype(BF)
+        parts[c, h] = dot(jnp.concatenate([scores[c, h], tails], axis=0), solved[c, h])
+    for c, h in both_of:
+        factor = gates_of[c][4]
+        rows, span_cols = slice(c * CHUNK, (c + 1) * CHUNK), slice(h * DK, (h + 1) * DK)
+        part = parts[c, h]
+        lifted = factor[:, h:h + 1] * queries[c, h // repeat] - part[:CHUNK, :DK]
+        state = carry[h]
+        left = jnp.concatenate([lifted, -part[CHUNK:, :DK]], axis=0).astype(BF)
+        moved = dot(left, state.astype(BF))
+        last = factor[CHUNK - 1:, h:h + 1]
+        out_ref[rows, span_cols] = moved[:CHUNK, DK:] + part[:CHUNK, DK:]
+        lift_ref[rows, span_cols] = moved[:CHUNK, :DK].astype(BF)
+        fresh_state = last * state + moved[CHUNK:]
+        carry[h, :, :DK] = fresh_state[:, :DK]
+        carry[h, :, DK:] = fresh_state[:, DK:] + part[CHUNK:, DK:]
 
     @pl.when(step == pl.num_programs(0) - 1)
     def _():
-        parts = map_ref.shape[0] // value_heads
-        width = DK // parts
+        pieces = map_ref.shape[0] // value_heads
+        width = DK // pieces
         for h in heads:
             moves = (carry[h, :, :DK] - ident).astype(BF)
             ends = carry[h, :, DK:].T.astype(BF)
-            for p in range(parts):
-                map_ref[h * parts + p, :DK] = moves
-                map_ref[h * parts + p, DK:] = ends[p * width:(p + 1) * width]
+            for p in range(pieces):
+                map_ref[h * pieces + p, :DK] = moves
+                map_ref[h * pieces + p, DK:] = ends[p * width:(p + 1) * width]
 
 
 def run_blocks(x, weights, rate, shift, key_heads, value_heads, span, takers):
@@ -420,6 +430,7 @@
     r_out, r_lifted, _ = run_blocks(
         tokens, weights, rate, shift, key_heads, value_heads, length // ROWS, value_heads
     )
+    maps, r_out, r_lifted = lax.optimization_barrier((maps, r_out, r_lifted))
     states = lax.all_to_all(run_scan(maps), "seq", split_axis=0, concat_axis=0, tiled=True)
     start = states[:, 0].reshape(value_heads, DK, DK)
     end = states[:, 1].reshape(value_heads, DK, DK)

time: 203 us -> 187 us (0.921)
  Pallas kernels: 128 us -> 114 us
  blocking collectives: 26 us -> 19.5 us
  starting transfers between devices: 8.37 us -> 11.9 us
    pallas_call x2, Pallas kernels: 65.5 us -> 51.7 us  [run_blocks(): pl.pallas_call(functools.partial(block_kernel, key_heads, value_heads, sp...]
    all_to_all x1, blocking collectives: 26 us -> 19.5 us  [shards(): lax.all_to_all(run_scan(maps), 'seq', split_axis=0, concat_axis=0, tiled=...]
    all_to_all x1, starting transfers between devices: 4.75 us -> 7.41 us  [shards(): lax.all_to_all(own_map, 'seq', split_axis=0, concat_axis=0, tiled=True)]
    unnamed x16 -> x18, local copies, waits for them, and re-layouts: 8.28 us -> 8.55 us
  transfers between devices with their start and end apart: 3 -> 3, of which waited for: 1 -> 1; matrix products, arithmetic and copies ran while one was open for 2% -> 3% of each run, Pallas kernels for 63% -> 59%
where the time goes in v4:
time: 187 us; the launch traced here: 186 us
  Pallas kernels  114 us (61%)
  blocking collectives  19.5 us (10%)
  local copies, waits for them, and re-layouts  15.2 us (8%)
  between operations  14.8 us (8%)
  starting transfers between devices  11.9 us (6%)
  waiting for transfers between devices  9.46 us (5%)
    pallas_call x1, Pallas kernels, run_gather(): pl.pallas_call(functools.partial(gather_kernel, count), out_shape=jax.Sha...  54.8 us
    pallas_call x2, Pallas kernels, run_blocks(): pl.pallas_call(functools.partial(block_kernel, key_heads, value_heads, sp...  51.7 us
    all_to_all x1, blocking collectives, shards(): lax.all_to_all(run_scan(maps), 'seq', split_axis=0, concat_axis=0, tiled=...  19.5 us
    all_to_all x1, waiting for transfers between devices, shards(): lax.all_to_all(r_done, 'grp', split_axis=0, concat_axis=0, tiled=True)  8.76 us
    unnamed x18, local copies, waits for them, and re-layouts  8.55 us
    all_to_all x1, starting transfers between devices, shards(): lax.all_to_all(own_map, 'seq', split_axis=0, concat_axis=0, tiled=True)  7.41 us
    pallas_call x2, Pallas kernels, run_finish(): pl.pallas_call(finish_kernel, grid=(count // ROWS,), in_specs=[rows, rows...  5.04 us
    all_to_all x1, starting transfers between devices, shards(): lax.all_to_all(r_done, 'grp', split_axis=0, concat_axis=0, tiled=True)  4.42 us
  transfers between devices with their start and end apart: 3, of which 1 were waited for; matrix products, arithmetic and copies ran while one was open for 3% of the time, Pallas kernels for 59%

profile of v4, /device:TPU:8, one launch (start us, length us, event | category | flops | bytes accessed | tf_op | source)
XLA Modules:
  0.0 185.6 jit_solution(10944390236919486112)
XLA Ops:
  7.2 0.0 all-gather.3.cloned.1.call-start
  7.2 0.7 all-gather.3.cloned.1.call-update
  7.9 0.7 dynamic_slice.6
  8.6 0.7 dynamic_slice.7
  9.4 0.8 copy.13
  10.2 0.8 copy.14
  11.0 1.9 %concatenate.3.own_ref = bf16[128,2176]{1,0:T(8,128)(2,1)} concatenate(bf16[128,512]{1,0:T(8,128)(2,1)} %param.13, bf16[128,512]{1,0:T(8,128)(2,1)} %param.14, bf16[128,1024]{1,0:T(8,128)(2,1)} %param.15, bf16[128,8]{1,0:T(8,128)(2,1)S(1)} %copy.13, bf16[128,8]{1,0:T(8,128)(2,1)S(1)} %copy.14, bf16[128,112]{1,0:T(8,128)(2,1)S(1)} %broadcast_in_dim.14), dimensions={1} | concatenate | bytes 1114112 | tf_op jit(solution)/shard_map/concatenate | solution.py:418
  12.9 54.8 %shard_map.122.w_ref = bf16[2048,2176]{1,0:T(8,128)(2,1)} custom-call(bf16[128,2176]{1,0:T(8,128)(2,1)} %concatenate.3.own_ref), custom_call_target="tpu_custom_call" | custom-call | bytes 35651584 | tf_op jit(solution)/shard_map/pallas_call | solution.py:345
  67.7 0.1 pad_bitcast_fusion
  67.8 33.2 %shard_map.123 = (f32[1024,1024]{1,0:T(8,128)}, bf16[1024,1024]{1,0:T(8,128)(2,1)S(1)}, bf16[16,192,128]{2,1,0:T(8,128)(2,1)S(1)}) custom-call(bf16[1024,2048]{1,0:T(8,128)(2,1)} %x_ref.1, bf16[2048,2176]{1,0:T(8,128)(2,1)} %shard_map.122.w_ref, f32[1,128]{1,0:T(1,128)S(1)} %get-tuple-element.21.rate_ref, f32[1,128]{1,0:T(1,128)S(1)} %get-tuple-element.20.shift_ref), custom_call_target="tpu_custom_call" | custom-call | flops 14579400704 | bytes 19398656 | tf_op jit(solution)/shard_map/pallas_call | solution.py:159
  101.0 0.0 copy-start.5
  101.0 0.9 copy-done.5
  101.9 7.4 %all-to-all-start = ((bf16[16,192,128]{2,1,0:T(8,128)(2,1)}), bf16[16,192,128]{2,1,0:T(8,128)(2,1)S(1)}, u32[]{:S(2)}, u32[]{:S(2)}) async-start(bf16[16,192,128]{2,1,0:T(8,128)(2,1)} %copy-done.5), calls=%async_computation | async-start | bytes 1572864 | tf_op jit(solution)/shard_map/all_to_all | solution.py:429
  109.3 0.0 all-gather.3.cloned.1.call-done
  109.3 0.0 copy-start.7
  109.3 1.6 copy-done.7
  110.9 18.5 %shard_map.124 = (f32[512,1024]{1,0:T(8,128)S(1)}, bf16[512,1024]{1,0:T(8,128)(2,1)S(1)}, bf16[8,256,128]{2,1,0:T(8,128)(2,1)}) custom-call(bf16[512,2048]{1,0:T(8,128)(2,1)S(1)} %bitcast.16, bf16[2048,2176]{1,0:T(8,128)(2,1)} %shard_map.122.w_ref, f32[1,128]{1,0:T(1,128)S(1)} %get-tuple-element.21.rate_ref, f32[1,128]{1,0:T(1,128)S(1)} %get-tuple-element.20.shift_ref), custom_call_target="tpu_custom_call" | custom-call | flops 7289700352 | bytes 14155776 | tf_op jit(solution)/shard_map/pallas_call | solution.py:159
  129.4 0.0 copy-start.1
  129.4 1.3 copy-done.1
  130.7 0.0 copy-start.3
  130.7 1.0 copy-done.3
  131.7 0.0 copy-start.6
  131.7 0.0 all-to-all-done.maps_ref
  131.7 0.0 copy-start.2
  131.7 0.0 copy-start.4
  131.7 2.1 %shard_map.125 = bf16[16,2,64,128]{3,2,1,0:T(8,128)(2,1)S(1)} custom-call(bf16[16,192,128]{2,1,0:T(8,128)(2,1)S(1)} %all-to-all-done.maps_ref), custom_call_target="tpu_custom_call" | custom-call | tf_op jit(solution)/shard_map/pallas_call | solution.py:208
  133.8 19.5 %all_to_all.15 = bf16[16,2,64,128]{3,2,1,0:T(8,128)(2,1)S(1)} all-to-all(bf16[16,2,64,128]{3,2,1,0:T(8,128)(2,1)S(1)} %shard_map.125), channel_id=1, replica_groups=mesh['seq'=16,'grp'=2] {'seq'}, dimensions={0} | all-to-all | bytes 1048576 | tf_op jit(solution)/shard_map/all_to_all | solution.py:434
  153.4 0.0 copy-done.6
  153.4 0.0 copy-done.2
  153.4 0.0 copy-done.4
  153.4 1.9 %shard_map.127 = bf16[512,1024]{1,0:T(8,128)(2,1)} custom-call(f32[512,1024]{1,0:T(8,128)S(1)} %copy-done.2, bf16[512,1024]{1,0:T(8,128)(2,1)S(1)} %copy-done.4, bf16[8,128,128]{2,1,0:T(8,128)(2,1)S(1)} %bitcast.13, f32[1,128]{1,0:T(1,128)S(1)} %bitcast.14), custom_call_target="tpu_custom_call" | custom-call | flops 134217728 | bytes 4194304 | tf_op jit(solution)/shard_map/pallas_call | solution.py:373
  155.3 4.4 %all-to-all-start.2 = ((bf16[2,256,1024]{2,1,0:T(8,128)(2,1)}), bf16[2,256,1024]{2,1,0:T(8,128)(2,1)}, u32[]{:S(2)}, u32[]{:S(2)}) async-start(bf16[2,256,1024]{2,1,0:T(8,128)(2,1)} %bitcast.7), calls=%async_computation.2 | async-start | bytes 2097152 | tf_op jit(solution)/shard_map/all_to_all | solution.py:439
  160.4 0.0 copy-start
  160.4 2.2 %copy-done = f32[1024,1024]{1,0:T(8,128)S(1)} copy-done((f32[1024,1024]{1,0:T(8,128)S(1)}, f32[1024,1024]{1,0:T(8,128)}, u32[]{:S(2)}) %copy-start) | copy-done | bytes 4194328
  162.6 3.2 %shard_map.126 = bf16[1024,1024]{1,0:T(8,128)(2,1)} custom-call(f32[1024,1024]{1,0:T(8,128)S(1)} %copy-done, bf16[1024,1024]{1,0:T(8,128)(2,1)S(1)} %get-tuple-element.11.lift_ref, bf16[8,128,128]{2,1,0:T(8,128)(2,1)S(1)} %bitcast.12, f32[1,128]{1,0:T(1,128)S(1)} %bitcast.15), custom_call_target="tpu_custom_call" | custom-call | flops 268435456 | bytes 8388608 | tf_op jit(solution)/shard_map/pallas_call | solution.py:373
  165.7 8.8 %all-to-all-done.2 = bf16[2,256,1024]{2,1,0:T(8,128)(2,1)} async-done(((bf16[2,256,1024]{2,1,0:T(8,128)(2,1)}), bf16[2,256,1024]{2,1,0:T(8,128)(2,1)}, u32[]{:S(2)}, u32[]{:S(2)}) %all-to-all-start.2) | async-done | bytes 1048608 | tf_op jit(solution)/shard_map/all_to_all | solution.py:439
  174.5 2.3 %copy.15 = bf16[256,2,1024]{2,1,0:T(2,128)(2,1)S(1)} copy(bf16[256,2,1024]{2,0,1:T(8,128)(2,1)} %bitcast.8) | data formatting | bytes 2097152 | tf_op jit(solution)/shard_map/transpose | solution.py:440
  176.8 0.8 reshape.66
  177.6 1.1 broadcast_select_fusion
  (3 shorter events, 0.0 us)
Async XLA Ops:
  7.2 102.1 %all-gather.3.cloned.1.call-start = ((), (), s32[]{:S(2)}) async-start(), calls=%async_computation.3 | async-start | bytes 3145728 | tf_op jit(solution)/shard_map/all_gather | solution.py:423
  101.0 0.9 copy-start.5
  101.9 29.9 %all-to-all-start = ((bf16[16,192,128]{2,1,0:T(8,128)(2,1)}), bf16[16,192,128]{2,1,0:T(8,128)(2,1)S(1)}, u32[]{:S(2)}, u32[]{:S(2)}) async-start(bf16[16,192,128]{2,1,0:T(8,128)(2,1)} %copy-done.5), calls=%async_computation | async-start | bytes 1572864 | tf_op jit(solution)/shard_map/all_to_all | solution.py:429
  109.3 1.6 copy-start.7
  129.4 1.3 copy-start.1
  130.7 1.0 copy-start.3
  131.7 21.7 %copy-start.6 = (f32[128]{0:T(128)S(1)}, f32[128]{0:T(128)}, u32[]{:S(2)}) copy-start(f32[128]{0:T(128)} %param.20) | copy-start | bytes 1540
  131.7 21.7 %copy-start.2 = (f32[512,1024]{1,0:T(8,128)S(1)}, f32[512,1024]{1,0:T(8,128)}, u32[]{:S(2)}) copy-start(f32[512,1024]{1,0:T(8,128)} %copy-done.1) | copy-start | bytes 6291460
  131.7 21.7 %copy-start.4 = (bf16[512,1024]{1,0:T(8,128)(2,1)S(1)}, bf16[512,1024]{1,0:T(8,128)(2,1)}, u32[]{:S(2)}) copy-start(bf16[512,1024]{1,0:T(8,128)(2,1)} %copy-done.3) | copy-start | bytes 3145732
  155.3 19.2 %all-to-all-start.2 = ((bf16[2,256,1024]{2,1,0:T(8,128)(2,1)}), bf16[2,256,1024]{2,1,0:T(8,128)(2,1)}, u32[]{:S(2)}, u32[]{:S(2)}) async-start(bf16[2,256,1024]{2,1,0:T(8,128)(2,1)} %bitcast.7), calls=%async_computation.2 | async-start | bytes 2097152 | tf_op jit(solution)/shard_map/all_to_all | solution.py:439
  160.4 2.2 %copy-start = (f32[1024,1024]{1,0:T(8,128)S(1)}, f32[1024,1024]{1,0:T(8,128)}, u32[]{:S(2)}) copy-start(f32[1024,1024]{1,0:T(8,128)} %get-tuple-element.10.out_ref) | copy-start | bytes 12582916
Sparse Core Ops, SparseCore 0:
  9.5 34.2 all-gather.2

commit v5 on v4

--- a/solution.py
+++ b/solution.py
@@ -57,7 +57,7 @@
         )
         size *= 2
 
-    chunks = range(ROWS // CHUNK)
+    chunks = range(x_ref.shape[0] // CHUNK)
     both_of = [(c, h) for c in chunks for h in heads]
     gates_of, queries, keys, keys_t, dots = [], {}, {}, {}, {}
     for c in chunks:
@@ -150,7 +150,7 @@
                 map_ref[h * pieces + p, DK:] = ends[p * width:(p + 1) * width]
 
 
-def run_blocks(x, weights, rate, shift, key_heads, value_heads, span, takers):
+def run_blocks(x, weights, rate, shift, key_heads, value_heads, span, takers, tall):
     count, depth = x.shape
     total = weights.shape[1]
     width = value_heads * DK
@@ -158,16 +158,16 @@
     whole = lambda shape: pl.BlockSpec(shape, lambda i: (0,) * len(shape))
     return pl.pallas_call(
         functools.partial(block_kernel, key_heads, value_heads, span),
-        grid=(count // ROWS,),
+        grid=(count // tall,),
         in_specs=[
-            pl.BlockSpec((ROWS, depth), lambda i: (i, 0)),
+            pl.BlockSpec((tall, depth), lambda i: (i, 0)),
             pl.BlockSpec((depth, total), lambda i: (0, 0), pipeline_mode=pl.Buffered(1)),
             whole((1, LANES)),
             whole((1, LANES)),
         ],
         out_specs=[
-            pl.BlockSpec((ROWS, width), lambda i: (i, 0)),
-            pl.BlockSpec((ROWS, width), lambda i: (i, 0)),
+            pl.BlockSpec((tall, width), lambda i: (i, 0)),
+            pl.BlockSpec((tall, width), lambda i: (i, 0)),
             whole((takers, map_rows, DK)),
         ],
         out_shape=[
@@ -176,7 +176,7 @@
             jax.ShapeDtypeStruct((takers, map_rows, DK), BF),
         ],
         scratch_shapes=[
-            pltpu.VMEM((ROWS, total), F32),
+            pltpu.VMEM((tall, total), F32),
             pltpu.VMEM((value_heads, DK, 2 * DK), F32),
         ],
         compiler_params=pltpu.CompilerParams(
@@ -422,13 +422,14 @@
     length, depth = response_tokens.shape[2:]
     tokens = lax.all_gather(response_tokens.reshape(length, depth), "grp", axis=0, tiled=True)
 
-    blocks = prompt_tokens.shape[0] // ROWS
+    tall = 2 * ROWS if prompt_tokens.shape[0] % (2 * ROWS) == 0 else ROWS
+    blocks = prompt_tokens.shape[0] // tall
     out, lifted, own_map = run_blocks(
-        prompt_tokens, weights, rate, shift, key_heads, value_heads, blocks, n_seq
+        prompt_tokens, weights, rate, shift, key_heads, value_heads, blocks, n_seq, tall
     )
     maps = lax.all_to_all(own_map, "seq", split_axis=0, concat_axis=0, tiled=True)
     r_out, r_lifted, _ = run_blocks(
-        tokens, weights, rate, shift, key_heads, value_heads, length // ROWS, value_heads
+        tokens, weights, rate, shift, key_heads, value_heads, length // ROWS, value_heads, ROWS
     )
     maps, r_out, r_lifted = lax.optimization_barrier((maps, r_out, r_lifted))
     states = lax.all_to_all(run_scan(maps), "seq", split_axis=0, concat_axis=0, tiled=True)

time: 187 us -> 189 us (1.011)
  no operation moved by 1% of the time
where the time goes in v5:
time: 189 us; the launch traced here: 187 us
  Pallas kernels  115 us (61%)
  blocking collectives  19.5 us (10%)
  local copies, waits for them, and re-layouts  15.2 us (8%)
  between operations  14.8 us (8%)
  starting transfers between devices  11.9 us (6%)
  waiting for transfers between devices  9.45 us (5%)
    pallas_call x1, Pallas kernels, run_gather(): pl.pallas_call(functools.partial(gather_kernel, count), out_shape=jax.Sha...  54.8 us
    pallas_call x2, Pallas kernels, run_blocks(): pl.pallas_call(functools.partial(block_kernel, key_heads, value_heads, sp...  53 us
    all_to_all x1, blocking collectives, shards(): lax.all_to_all(run_scan(maps), 'seq', split_axis=0, concat_axis=0, tiled=...  19.5 us
    all_to_all x1, waiting for transfers between devices, shards(): lax.all_to_all(r_done, 'grp', split_axis=0, concat_axis=0, tiled=True)  8.76 us
    unnamed x18, local copies, waits for them, and re-layouts  8.55 us
    all_to_all x1, starting transfers between devices, shards(): lax.all_to_all(own_map, 'seq', split_axis=0, concat_axis=0, tiled=True)  7.41 us
    pallas_call x2, Pallas kernels, run_finish(): pl.pallas_call(finish_kernel, grid=(count // ROWS,), in_specs=[rows, rows...  5.04 us
    all_to_all x1, starting transfers between devices, shards(): lax.all_to_all(r_done, 'grp', split_axis=0, concat_axis=0, tiled=True)  4.42 us
  transfers between devices with their start and end apart: 3, of which 1 were waited for; matrix products, arithmetic and copies ran while one was open for 3% of the time, Pallas kernels for 59%

profile of v5, /device:TPU:8, one launch (start us, length us, event | category | flops | bytes accessed | tf_op | source)
XLA Modules:
  0.0 186.9 jit_solution(8896535145673891786)
XLA Ops:
  7.2 0.0 all-gather.3.cloned.1.call-start
  7.2 0.7 all-gather.3.cloned.1.call-update
  7.9 0.7 dynamic_slice.6
  8.6 0.7 dynamic_slice.7
  9.4 0.8 copy.13
  10.2 0.8 copy.14
  11.0 1.9 %concatenate.3.own_ref = bf16[128,2176]{1,0:T(8,128)(2,1)} concatenate(bf16[128,512]{1,0:T(8,128)(2,1)} %param.13, bf16[128,512]{1,0:T(8,128)(2,1)} %param.14, bf16[128,1024]{1,0:T(8,128)(2,1)} %param.15, bf16[128,8]{1,0:T(8,128)(2,1)S(1)} %copy.13, bf16[128,8]{1,0:T(8,128)(2,1)S(1)} %copy.14, bf16[128,112]{1,0:T(8,128)(2,1)S(1)} %broadcast_in_dim.14), dimensions={1} | concatenate | bytes 1114112 | tf_op jit(solution)/shard_map/concatenate | solution.py:418
  12.9 54.8 %shard_map.122.w_ref = bf16[2048,2176]{1,0:T(8,128)(2,1)} custom-call(bf16[128,2176]{1,0:T(8,128)(2,1)} %concatenate.3.own_ref), custom_call_target="tpu_custom_call" | custom-call | bytes 35651584 | tf_op jit(solution)/shard_map/pallas_call | solution.py:345
  67.7 0.1 pad_bitcast_fusion
  67.8 34.5 %shard_map.123 = (f32[1024,1024]{1,0:T(8,128)}, bf16[1024,1024]{1,0:T(8,128)(2,1)S(1)}, bf16[16,192,128]{2,1,0:T(8,128)(2,1)S(1)}) custom-call(bf16[1024,2048]{1,0:T(8,128)(2,1)} %x_ref.1, bf16[2048,2176]{1,0:T(8,128)(2,1)} %shard_map.122.w_ref, f32[1,128]{1,0:T(1,128)S(1)} %get-tuple-element.21.rate_ref, f32[1,128]{1,0:T(1,128)S(1)} %get-tuple-element.20.shift_ref), custom_call_target="tpu_custom_call" | custom-call | flops 14579400704 | bytes 19398656 | tf_op jit(solution)/shard_map/pallas_call | solution.py:159
  102.3 0.0 copy-start.5
  102.3 0.9 copy-done.5
  103.2 7.4 %all-to-all-start = ((bf16[16,192,128]{2,1,0:T(8,128)(2,1)}), bf16[16,192,128]{2,1,0:T(8,128)(2,1)S(1)}, u32[]{:S(2)}, u32[]{:S(2)}) async-start(bf16[16,192,128]{2,1,0:T(8,128)(2,1)} %copy-done.5), calls=%async_computation | async-start | bytes 1572864 | tf_op jit(solution)/shard_map/all_to_all | solution.py:430
  110.6 0.0 all-gather.3.cloned.1.call-done
  110.6 0.0 copy-start.7
  110.6 1.6 copy-done.7
  112.2 18.5 %shard_map.124 = (f32[512,1024]{1,0:T(8,128)S(1)}, bf16[512,1024]{1,0:T(8,128)(2,1)S(1)}, bf16[8,256,128]{2,1,0:T(8,128)(2,1)}) custom-call(bf16[512,2048]{1,0:T(8,128)(2,1)S(1)} %bitcast.16, bf16[2048,2176]{1,0:T(8,128)(2,1)} %shard_map.122.w_ref, f32[1,128]{1,0:T(1,128)S(1)} %get-tuple-element.21.rate_ref, f32[1,128]{1,0:T(1,128)S(1)} %get-tuple-element.20.shift_ref), custom_call_target="tpu_custom_call" | custom-call | flops 7289700352 | bytes 14155776 | tf_op jit(solution)/shard_map/pallas_call | solution.py:159
  130.7 0.0 copy-start.1
  130.7 1.3 copy-done.1
  132.1 0.0 copy-start.3
  132.1 1.0 copy-done.3
  133.0 0.0 copy-start.6
  133.0 0.0 all-to-all-done.maps_ref
  133.0 0.0 copy-start.2
  133.0 0.0 copy-start.4
  133.0 2.1 %shard_map.125 = bf16[16,2,64,128]{3,2,1,0:T(8,128)(2,1)S(1)} custom-call(bf16[16,192,128]{2,1,0:T(8,128)(2,1)S(1)} %all-to-all-done.maps_ref), custom_call_target="tpu_custom_call" | custom-call | tf_op jit(solution)/shard_map/pallas_call | solution.py:208
  135.2 19.5 %all_to_all.15 = bf16[16,2,64,128]{3,2,1,0:T(8,128)(2,1)S(1)} all-to-all(bf16[16,2,64,128]{3,2,1,0:T(8,128)(2,1)S(1)} %shard_map.125), channel_id=1, replica_groups=mesh['seq'=16,'grp'=2] {'seq'}, dimensions={0} | all-to-all | bytes 1048576 | tf_op jit(solution)/shard_map/all_to_all | solution.py:435
  154.7 0.0 copy-done.6
  154.7 0.0 copy-done.2
  154.7 0.0 copy-done.4
  154.8 1.9 %shard_map.127 = bf16[512,1024]{1,0:T(8,128)(2,1)} custom-call(f32[512,1024]{1,0:T(8,128)S(1)} %copy-done.2, bf16[512,1024]{1,0:T(8,128)(2,1)S(1)} %copy-done.4, bf16[8,128,128]{2,1,0:T(8,128)(2,1)S(1)} %bitcast.13, f32[1,128]{1,0:T(1,128)S(1)} %bitcast.14), custom_call_target="tpu_custom_call" | custom-call | flops 134217728 | bytes 4194304 | tf_op jit(solution)/shard_map/pallas_call | solution.py:373
  156.6 4.4 %all-to-all-start.2 = ((bf16[2,256,1024]{2,1,0:T(8,128)(2,1)}), bf16[2,256,1024]{2,1,0:T(8,128)(2,1)}, u32[]{:S(2)}, u32[]{:S(2)}) async-start(bf16[2,256,1024]{2,1,0:T(8,128)(2,1)} %bitcast.7), calls=%async_computation.2 | async-start | bytes 2097152 | tf_op jit(solution)/shard_map/all_to_all | solution.py:440
  161.7 0.0 copy-start
  161.7 2.2 %copy-done = f32[1024,1024]{1,0:T(8,128)S(1)} copy-done((f32[1024,1024]{1,0:T(8,128)S(1)}, f32[1024,1024]{1,0:T(8,128)}, u32[]{:S(2)}) %copy-start) | copy-done | bytes 4194328
  163.9 3.2 %shard_map.126 = bf16[1024,1024]{1,0:T(8,128)(2,1)} custom-call(f32[1024,1024]{1,0:T(8,128)S(1)} %copy-done, bf16[1024,1024]{1,0:T(8,128)(2,1)S(1)} %get-tuple-element.11.lift_ref, bf16[8,128,128]{2,1,0:T(8,128)(2,1)S(1)} %bitcast.12, f32[1,128]{1,0:T(1,128)S(1)} %bitcast.15), custom_call_target="tpu_custom_call" | custom-call | flops 268435456 | bytes 8388608 | tf_op jit(solution)/shard_map/pallas_call | solution.py:373
  167.1 8.8 %all-to-all-done.2 = bf16[2,256,1024]{2,1,0:T(8,128)(2,1)} async-done(((bf16[2,256,1024]{2,1,0:T(8,128)(2,1)}), bf16[2,256,1024]{2,1,0:T(8,128)(2,1)}, u32[]{:S(2)}, u32[]{:S(2)}) %all-to-all-start.2) | async-done | bytes 1048608 | tf_op jit(solution)/shard_map/all_to_all | solution.py:440
  175.8 2.3 %copy.15 = bf16[256,2,1024]{2,1,0:T(2,128)(2,1)S(1)} copy(bf16[256,2,1024]{2,0,1:T(8,128)(2,1)} %bitcast.8) | data formatting | bytes 2097152 | tf_op jit(solution)/shard_map/transpose | solution.py:441
  178.1 0.8 reshape.66
  179.0 1.1 broadcast_select_fusion
  (3 shorter events, 0.0 us)
Async XLA Ops:
  7.2 103.4 %all-gather.3.cloned.1.call-start = ((), (), s32[]{:S(2)}) async-start(), calls=%async_computation.3 | async-start | bytes 3145728 | tf_op jit(solution)/shard_map/all_gather | solution.py:423
  102.3 0.9 copy-start.5
  103.2 29.9 %all-to-all-start = ((bf16[16,192,128]{2,1,0:T(8,128)(2,1)}), bf16[16,192,128]{2,1,0:T(8,128)(2,1)S(1)}, u32[]{:S(2)}, u32[]{:S(2)}) async-start(bf16[16,192,128]{2,1,0:T(8,128)(2,1)} %copy-done.5), calls=%async_computation | async-start | bytes 1572864 | tf_op jit(solution)/shard_map/all_to_all | solution.py:430
  110.6 1.6 copy-start.7
  130.7 1.3 copy-start.1
  132.1 1.0 copy-start.3
  133.0 21.7 %copy-start.6 = (f32[128]{0:T(128)S(1)}, f32[128]{0:T(128)}, u32[]{:S(2)}) copy-start(f32[128]{0:T(128)} %param.20) | copy-start | bytes 1540
  133.0 21.7 %copy-start.2 = (f32[512,1024]{1,0:T(8,128)S(1)}, f32[512,1024]{1,0:T(8,128)}, u32[]{:S(2)}) copy-start(f32[512,1024]{1,0:T(8,128)} %copy-done.1) | copy-start | bytes 6291460
  133.0 21.7 %copy-start.4 = (bf16[512,1024]{1,0:T(8,128)(2,1)S(1)}, bf16[512,1024]{1,0:T(8,128)(2,1)}, u32[]{:S(2)}) copy-start(bf16[512,1024]{1,0:T(8,128)(2,1)} %copy-done.3) | copy-start | bytes 3145732
  156.6 19.2 %all-to-all-start.2 = ((bf16[2,256,1024]{2,1,0:T(8,128)(2,1)}), bf16[2,256,1024]{2,1,0:T(8,128)(2,1)}, u32[]{:S(2)}, u32[]{:S(2)}) async-start(bf16[2,256,1024]{2,1,0:T(8,128)(2,1)} %bitcast.7), calls=%async_computation.2 | async-start | bytes 2097152 | tf_op jit(solution)/shard_map/all_to_all | solution.py:440
  161.7 2.2 %copy-start = (f32[1024,1024]{1,0:T(8,128)S(1)}, f32[1024,1024]{1,0:T(8,128)}, u32[]{:S(2)}) copy-start(f32[1024,1024]{1,0:T(8,128)} %get-tuple-element.10.out_ref) | copy-start | bytes 12582916
Sparse Core Ops, SparseCore 0:
  9.5 34.2 all-gather.2
